TPU v7x, 256 devices: a whole 4x4x8 slice. The times are simulated.
256 devices in a mesh: dap: 64 (over z_lo, y, x, core), grp: 4 (over z_hi).
Axes of the slice: x: 4, y: 4, z: 8 (z_hi: 4, z_lo: 2; z = z_hi * 2 + z_lo), core: 2. Of those that a mesh axis runs over, the one named last changes fastest.
Arguments:
- pair_map: bfloat16 [512, 512, 128], P(('dap', 'grp')), may hold values from -6 to 6
- pair_mask: int32 [512, 512], P(('dap', 'grp')), may hold values 0 or 1
- edge_weights: bfloat16 [2, 128, 512], replicated, may hold values from -0.5 to 0.5
- gate_weights: bfloat16 [2, 128, 128], replicated, may hold values from -0.5 to 0.5
- out_weights: bfloat16 [2, 128, 128], replicated, may hold values from -0.5 to 0.5
- norm_gains: float32 [2, 2, 128], replicated, may hold values from 0.1 to 1.9
Outputs:
- updated: bfloat16 [512, 512, 128], P(('dap', 'grp'))
All inputs are finite; a program needn't handle non-finite values. No bound on the sum of `pair_mask` on one device may be relied on, other than what follows from the above.
Results may differ from a plain program's by a relative error of at most 0.018.
Values may be sent and summed in bfloat16 or wider, within the bound.
A program may use at most 64 MiB of HBM per device.

v0:
```python
import jax
import jax.numpy as jnp
from jax import lax
from jax.sharding import PartitionSpec as P


def normalize(values, axis):
    average = jnp.mean(values, axis=axis, keepdims=True)
    centred = values - average
    variance = jnp.mean(centred * centred, axis=axis, keepdims=True)
    return centred * lax.rsqrt(variance + 1e-05)


def per_device(pair_map, pair_mask, edge_weights, gate_weights, out_weights, norm_gains):
    rows_here, residues, width = (pair_map.shape[0], pair_map.shape[1], pair_map.shape[2])
    hidden = edge_weights.shape[2] // 4
    dap_size = lax.axis_size("dap")
    grp_size = lax.axis_size("grp")
    channels = hidden // dap_size
    mask_rows = pair_mask.astype(jnp.float32)

    def edge_maps(current, layer_idx, regroup_left):
        normed = (normalize(current.astype(jnp.float32), 2) * norm_gains[layer_idx, 0]).astype(
            jnp.bfloat16
        )
        weights = edge_weights[layer_idx]
        if regroup_left:
            source = (
                normed.reshape(rows_here, dap_size, grp_size, rows_here, width)
                .transpose(0, 2, 1, 3, 4)
                .reshape(rows_here, residues, width)
            )
            left_mask = (
                mask_rows.reshape(rows_here, dap_size, grp_size, rows_here)
                .transpose(0, 2, 1, 3)
                .reshape(rows_here, residues)
            )
        else:
            source = normed
            left_mask = mask_rows
        left_proj = jnp.einsum(
            "rnc,ch->hrn", source, weights[:, : 2 * hidden], preferred_element_type=jnp.float32
        )
        right_proj = jnp.einsum(
            "rnc,ch->hrn", normed, weights[:, 2 * hidden :], preferred_element_type=jnp.float32
        )
        left_edges = (
            jax.nn.sigmoid(left_proj[:hidden]) * left_proj[hidden:] * left_mask[None]
        ).astype(jnp.bfloat16)
        right_edges = (
            jax.nn.sigmoid(right_proj[:hidden]) * right_proj[hidden:] * mask_rows[None]
        ).astype(jnp.bfloat16)
        left_edges, right_edges = (
            lax.all_to_all(left_edges, "dap", split_axis=0, concat_axis=1, tiled=True),
            lax.all_to_all(right_edges, "dap", split_axis=0, concat_axis=1, tiled=True),
        )
        return (normed, left_edges, right_edges)

    def finish(current, normed, product_map, layer_idx):
        merged = lax.all_to_all(
            product_map.astype(jnp.bfloat16), "dap", split_axis=0, concat_axis=1, tiled=True
        )
        scaled = (
            normalize(merged.astype(jnp.float32), 1) * norm_gains[layer_idx, 1][None, :, None]
        ).astype(jnp.bfloat16)
        projected = jnp.einsum(
            "rhn,hc->rnc", scaled, out_weights[layer_idx], preferred_element_type=jnp.float32
        )
        gating = jax.nn.sigmoid(
            jnp.einsum(
                "rnc,cd->rnd", normed, gate_weights[layer_idx], preferred_element_type=jnp.float32
            )
        )
        return (current.astype(jnp.float32) + gating * projected).astype(jnp.bfloat16)

    normed, left_edges, right_edges = edge_maps(pair_map, 0, False)
    gathered = lax.all_gather(right_edges, "grp", axis=1, tiled=True)
    gathered = (
        gathered.reshape(channels, grp_size, dap_size, rows_here, residues)
        .transpose(0, 2, 1, 3, 4)
        .reshape(channels, residues, residues)
    )
    product_map = jnp.einsum(
        "cik,cjk->icj", left_edges, gathered, preferred_element_type=jnp.float32
    )
    current = finish(pair_map, normed, product_map, 0)
    normed, regrouped, right_edges = edge_maps(current, 1, True)
    product_map = lax.psum_scatter(
        jnp.einsum(
            "cki,ckj->icj", regrouped, right_edges, preferred_element_type=jnp.float32
        ).astype(jnp.bfloat16),
        "grp",
        scatter_dimension=0,
        tiled=True,
    ).astype(jnp.float32)
    return finish(current, normed, product_map, 1)


def solution(mesh):
    return jax.shard_map(
        per_device,
        mesh=mesh,
        in_specs=(P(("dap", "grp"), None, None), P(("dap", "grp"), None), P(), P(), P(), P()),
        out_specs=P(("dap", "grp"), None, None),
        check_vma=False,
    )
```

profile of v0, /device:TPU:1, one launch (start us, length us, event | category | flops | bytes accessed | tf_op | source)
XLA Modules:
  0.0 180.6 jit_solution(2637994322660297709)
XLA Ops:
  6.5 1.2 convert_reduce_fusion
  7.7 1.3 fusion.14
  9.1 0.8 slice_bitcast_fusion.10
  9.8 1.0 slice_bitcast_fusion
  10.8 0.5 convolution_bitcast_fusion.2
  11.3 0.5 convolution_bitcast_fusion.3
  11.8 0.3 fusion.28
  12.1 0.2 copy.38
  12.3 19.9 %all_to_all.90 = bf16[128,2,512]{2,1,0:T(2,128)(2,1)S(1)} all-to-all(bf16[128,2,512]{2,1,0:T(2,128)(2,1)S(1)} %copy.38), channel_id=1, replica_groups=mesh['dap'=64,'grp'=4] {'dap'}, dimensions={0} | all-to-all | bytes 524288 | tf_op jit(solution)/shard_map/all_to_all | solution.py:55
  32.2 0.9 copy.39
  33.1 0.0 all-gather.2.cloned.1.call-update
  33.1 0.2 copy.41
  33.3 14.0 %all_to_all.91 = bf16[128,2,512]{2,1,0:T(2,128)(2,1)S(1)} all-to-all(bf16[128,2,512]{2,1,0:T(2,128)(2,1)S(1)} %copy.41), channel_id=1, replica_groups=mesh['dap'=64,'grp'=4] {'dap'}, dimensions={0} | all-to-all | bytes 524288 | tf_op jit(solution)/shard_map/all_to_all | solution.py:54
  47.3 0.2 copy.42
  47.5 0.1 all_to_all.73
  47.6 18.6 %all-gather.2.cloned.1.call-done = bf16[2,512,512]{2,0,1:T(2,128)(2,1)} async-done(((bf16[2,128,512]{2,0,1:T(2,128)(2,1)}), bf16[2,512,512]{2,0,1:T(2,128)(2,1)}) %all-gather.2.cloned.1.call-update) | async-done | bytes 1048592 | tf_op jit(solution)/shard_map/all_gather | solution.py:77
  66.2 2.0 %copy.40 = bf16[2,64,4,2,512]{4,3,2,1,0:T(2,128)(2,1)S(1)} copy(bf16[2,64,4,2,512]{4,0,3,1,2:T(2,128)(2,1)} %bitcast.131) | data formatting | bytes 2097152 | tf_op jit(solution)/shard_map/transpose | solution.py:80
  68.2 0.4 reshape.78
  68.7 0.4 fusion.11
  69.1 0.0 copy-start.3
  69.1 0.9 copy.43
  70.0 8.5 %all-to-all-start.2 = ((bf16[128,2,512]{2,1,0:T(2,128)(2,1)}), bf16[128,2,512]{2,1,0:T(2,128)(2,1)S(1)}, u32[]{:S(2)}, u32[]{:S(2)}) async-start(bf16[128,2,512]{2,1,0:T(2,128)(2,1)} %copy.43), calls=%async_computation.2 | async-start | bytes 524288 | tf_op jit(solution)/shard_map/all_to_all | solution.py:60
  78.5 0.3 reshape.81
  78.9 0.1 mul.152
  79.0 0.2 mul.165
  79.2 0.5 fusion.5
  79.7 8.6 %all-to-all-done.2 = bf16[128,2,512]{2,1,0:T(2,128)(2,1)S(1)} async-done(((bf16[128,2,512]{2,1,0:T(2,128)(2,1)}), bf16[128,2,512]{2,1,0:T(2,128)(2,1)S(1)}, u32[]{:S(2)}, u32[]{:S(2)}) %all-to-all-start.2) | async-done | bytes 262176 | tf_op jit(solution)/shard_map/all_to_all | solution.py:60
  88.3 0.2 fusion.45
  88.5 0.4 fusion.48
  88.9 0.4 fusion.50
  89.3 0.2 copy.44
  89.5 0.4 fusion.65
  90.0 0.4 multiply_reduce_fusion
  90.4 0.3 multiply_convert_fusion
  90.7 0.2 copy.48
  90.9 0.3 convolution_bitcast_fusion
  91.2 0.2 fusion.18
  91.4 0.9 copy.50
  92.3 4.5 %all-to-all-start.4 = ((bf16[128,2,512]{2,1,0:T(2,128)(2,1)}), bf16[128,2,512]{2,1,0:T(2,128)(2,1)S(1)}, u32[]{:S(2)}, u32[]{:S(2)}) async-start(bf16[128,2,512]{2,1,0:T(2,128)(2,1)} %copy.50), calls=%async_computation.4 | async-start | bytes 524288 | tf_op jit(solution)/shard_map/all_to_all | solution.py:54
  96.8 0.3 convolution_bitcast_fusion.1
  97.0 0.2 fusion.23
  97.3 0.9 copy.46
  98.1 8.5 %all-to-all-done.4 = bf16[128,2,512]{2,1,0:T(2,128)(2,1)S(1)} async-done(((bf16[128,2,512]{2,1,0:T(2,128)(2,1)}), bf16[128,2,512]{2,1,0:T(2,128)(2,1)S(1)}, u32[]{:S(2)}, u32[]{:S(2)}) %all-to-all-start.4) | async-done | bytes 262176 | tf_op jit(solution)/shard_map/all_to_all | solution.py:54
  106.6 4.5 %all-to-all-start.3 = ((bf16[128,2,512]{2,1,0:T(2,128)(2,1)}), bf16[128,2,512]{2,1,0:T(2,128)(2,1)S(1)}, u32[]{:S(2)}, u32[]{:S(2)}) async-start(bf16[128,2,512]{2,1,0:T(2,128)(2,1)} %copy.46), calls=%async_computation.3 | async-start | bytes 524288 | tf_op jit(solution)/shard_map/all_to_all | solution.py:55
  111.1 0.0 reduce-scatter.4.cloned.1.call-start
  111.1 0.2 copy.51
  111.3 0.1 all_to_all.82
  111.4 9.5 %all-to-all-done.3 = bf16[128,2,512]{2,1,0:T(2,128)(2,1)S(1)} async-done(((bf16[128,2,512]{2,1,0:T(2,128)(2,1)}), bf16[128,2,512]{2,1,0:T(2,128)(2,1)S(1)}, u32[]{:S(2)}, u32[]{:S(2)}) %all-to-all-start.3) | async-done | bytes 262176 | tf_op jit(solution)/shard_map/all_to_all | solution.py:55
  120.9 0.2 copy.47
  121.1 0.5 convolution_convert_fusion
  121.6 1.3 copy.58
  122.9 0.0 reduce-scatter.4.cloned.1.call-update
  123.0 28.2 %reduce-scatter.4.cloned.1.call-done = bf16[128,1024]{1,0:T(8,128)(2,1)} async-done(((bf16[512,1024]{1,0:T(8,128)(2,1)}), bf16[128,1024]{1,0:T(8,128)(2,1)}) %reduce-scatter.4.cloned.1.call-update) | async-done | bytes 262160
  151.2 1.1 copy.59
  152.3 0.9 copy.53
  153.2 8.6 %all-to-all-start.5 = ((bf16[128,2,512]{2,1,0:T(2,128)(2,1)}), bf16[128,2,512]{2,1,0:T(2,128)(2,1)S(1)}, u32[]{:S(2)}, u32[]{:S(2)}) async-start(bf16[128,2,512]{2,1,0:T(2,128)(2,1)} %copy.53), calls=%async_computation.5 | async-start | bytes 524288 | tf_op jit(solution)/shard_map/all_to_all | solution.py:60
  161.8 0.1 mul.171
  162.0 0.3 fusion.2
  162.3 9.3 %all-to-all-done.5 = bf16[128,2,512]{2,1,0:T(2,128)(2,1)S(1)} async-done(((bf16[128,2,512]{2,1,0:T(2,128)(2,1)}), bf16[128,2,512]{2,1,0:T(2,128)(2,1)S(1)}, u32[]{:S(2)}, u32[]{:S(2)}) %all-to-all-start.5) | async-done | bytes 262176 | tf_op jit(solution)/shard_map/all_to_all | solution.py:60
  171.6 0.2 fusion.38
  171.8 0.4 fusion.41
  172.2 0.4 fusion.43
  172.6 0.2 copy.54
  172.8 1.0 fusion.8
  (18 shorter events, 0.1 us)
Async XLA Ops:
  6.5 4.3 %copy-start = (bf16[2,512,128]{2,1,0:T(8,128)(2,1)S(1)}, bf16[2,512,128]{2,1,0:T(8,128)(2,1)}, u32[]{:S(2)}) copy-start(bf16[2,512,128]{2,1,0:T(8,128)(2,1)} %param.6) | copy-start | bytes 786436
  6.5 59.7 %all-gather.2.cloned.1.call-start = ((), (), s32[]{:S(2)}) async-start(), calls=%async_computation.7 | async-start | bytes 1310720 | tf_op jit(solution)/shard_map/all_gather | solution.py:77
  10.8 0.9 copy-start.2
  69.1 10.1 %copy-start.3 = (bf16[2,128,128]{2,1,0:T(8,128)(2,1)S(1)}, bf16[2,128,128]{2,1,0:T(8,128)(2,1)}, u32[]{:S(2)}) copy-start(bf16[2,128,128]{2,1,0:T(8,128)(2,1)} %param.9) | copy-start | bytes 196612
  70.0 18.3 %all-to-all-start.2 = ((bf16[128,2,512]{2,1,0:T(2,128)(2,1)}), bf16[128,2,512]{2,1,0:T(2,128)(2,1)S(1)}, u32[]{:S(2)}, u32[]{:S(2)}) async-start(bf16[128,2,512]{2,1,0:T(2,128)(2,1)} %copy.43), calls=%async_computation.2 | async-start | bytes 524288 | tf_op jit(solution)/shard_map/all_to_all | solution.py:60
  79.7 9.8 %copy-start.1 = (bf16[2,128,128]{2,1,0:T(8,128)(2,1)S(1)}, bf16[2,128,128]{2,1,0:T(8,128)(2,1)}, u32[]{:S(2)}) copy-start(bf16[2,128,128]{2,1,0:T(8,128)(2,1)} %param.10) | copy-start | bytes 196612
  92.3 14.3 %all-to-all-start.4 = ((bf16[128,2,512]{2,1,0:T(2,128)(2,1)}), bf16[128,2,512]{2,1,0:T(2,128)(2,1)S(1)}, u32[]{:S(2)}, u32[]{:S(2)}) async-start(bf16[128,2,512]{2,1,0:T(2,128)(2,1)} %copy.50), calls=%async_computation.4 | async-start | bytes 524288 | tf_op jit(solution)/shard_map/all_to_all | solution.py:54
  106.6 14.3 %all-to-all-start.3 = ((bf16[128,2,512]{2,1,0:T(2,128)(2,1)}), bf16[128,2,512]{2,1,0:T(2,128)(2,1)S(1)}, u32[]{:S(2)}, u32[]{:S(2)}) async-start(bf16[128,2,512]{2,1,0:T(2,128)(2,1)} %copy.46), calls=%async_computation.3 | async-start | bytes 524288 | tf_op jit(solution)/shard_map/all_to_all | solution.py:55
  111.1 40.1 %reduce-scatter.4.cloned.1.call-start = ((), (), s32[]{:S(2)}) async-start(), calls=%async_computation.8 | async-start | bytes 1310720
  153.2 18.4 %all-to-all-start.5 = ((bf16[128,2,512]{2,1,0:T(2,128)(2,1)}), bf16[128,2,512]{2,1,0:T(2,128)(2,1)S(1)}, u32[]{:S(2)}, u32[]{:S(2)}) async-start(bf16[128,2,512]{2,1,0:T(2,128)(2,1)} %copy.53), calls=%async_computation.5 | async-start | bytes 524288 | tf_op jit(solution)/shard_map/all_to_all | solution.py:60
Sparse Core Ops, SparseCore 0:
  33.2 32.9 all-gather.1
  123.1 28.0 reduce-scatter.3
where the time goes:
time: 181 us
  waiting for transfers between devices  82.6 us (46%)
  blocking collectives  33.9 us (19%)
  starting transfers between devices  26.2 us (14%)
  local copies, waits for them, and re-layouts  13.7 us (8%)
  between operations  13.7 us (8%)
  other arithmetic  5.97 us (3%)
  matrix products  4.57 us (3%)
    unnamed x3, waiting for transfers between devices  28.3 us
    all_to_all x1, blocking collectives, edge_maps(): lax.all_to_all(right_edges, 'dap', split_axis=0, concat_axis=1, tiled=True)  19.9 us
    all_gather x1, waiting for transfers between devices, per_device(): gathered = lax.all_gather(right_edges, 'grp', axis=1, tiled=True)  18.6 us
    all_to_all x2, waiting for transfers between devices, finish(): lax.all_to_all(product_map.astype(jnp.bfloat16), 'dap', split_axis=0, con...  17.9 us
    all_to_all x2, starting transfers between devices, finish(): lax.all_to_all(product_map.astype(jnp.bfloat16), 'dap', split_axis=0, con...  17.1 us
    all_to_all x1, blocking collectives, edge_maps(): lax.all_to_all(left_edges, 'dap', split_axis=0, concat_axis=1, tiled=True)  14 us
    all_to_all x1, waiting for transfers between devices, edge_maps(): lax.all_to_all(right_edges, 'dap', split_axis=0, concat_axis=1, tiled=True)  9.47 us
    all_to_all x1, waiting for transfers between devices, edge_maps(): lax.all_to_all(left_edges, 'dap', split_axis=0, concat_axis=1, tiled=True)  8.47 us
  transfers between devices with their start and end apart: 6, of which 6 were waited for; matrix products, arithmetic and copies ran while one was open for 2% of the time, Pallas kernels for 0%

commit v1 on v0

v1 whole, which is shorter than its diff:
```python
import functools

import jax
import jax.numpy as jnp
from jax import lax
from jax.experimental import pallas as pl
from jax.experimental.pallas import tpu as pltpu
from jax.sharding import PartitionSpec as P

BF = jnp.bfloat16
F32 = jnp.float32
MESH = pl.DeviceIdType.MESH


def dot(a, b, ca, cb):
    return lax.dot_general(a, b, (((ca,), (cb,)), ((), ())), preferred_element_type=F32)


def one_hot(source):
    rows = lax.broadcasted_iota(jnp.int32, (256, 256), 0)
    cols = lax.broadcasted_iota(jnp.int32, (256, 256), 1)
    return jnp.where(cols == source(rows), 1.0, 0.0).astype(BF)


def where_am_i():
    dap = lax.axis_index("dap")
    grp = lax.axis_index("grp")
    core = dap % 2
    x = (dap // 2) % 4
    y = (dap // 8) % 4
    zlo = dap // 32
    return x, y, zlo, grp, core


def device(x, y, zlo, zhi, core):
    return (((zlo * 4 + y) * 4 + x) * 2 + core, zhi)


def far_first(k, size):
    return (size // 2 + jnp.where(k % 2 == 1, size - (k + 1) // 2, k // 2)) % size


def kernel(z_ref, mask_ref, we_ref, wg_ref, wo_ref, gains_ref, out_ref,
           wt, perms, normed, cur, edges, send1, recv1, left, right, leftx, prod, send2, recv2, chan,
           s1, r1, s2, r2, sx, rx):
    x, y, zlo, zhi, core = where_am_i()
    slot = ((y * 4 + x) * 2 + core) * 4 + zhi
    channel = ((zlo * 4 + y) * 4 + x) * 4 + zhi
    sibling = device(x, y, zlo, zhi, 1 - core)

    barrier = pltpu.get_barrier_semaphore()

    def partner(i):
        tc, k = i % 2, i // 2
        tg = (zhi + far_first(k // 16, 4)) % 4
        tx = (x + far_first(k % 4, 4)) % 4
        ty = (y + far_first((k // 4) % 4, 4)) % 4
        return tx, ty, tg, tc

    def greet(i, carry):
        tx, ty, tg, tc = partner(i)

        @pl.when(jnp.logical_not((tx == x) & (ty == y) & (tg == zhi) & (zlo == core)))
        def _():
            pl.semaphore_signal(barrier, inc=1, device_id=device(tx, ty, core, tg, tc), device_id_type=MESH)

        return carry

    pl.semaphore_signal(barrier, inc=1, device_id=sibling, device_id_type=MESH)
    lax.fori_loop(0, 128, greet, 0)

    for u in range(2):
        wt[u] = we_ref[u].astype(F32).T.astype(BF)
    perms[0] = one_hot(lambda r: (r % 16) * 16 + r // 16)
    perms[1] = one_hot(lambda r: ((r // 2) % 16) * 16 + (r // 128) * 8 + (r % 2) * 4 + (r // 32) % 4)
    perms[2] = one_hot(lambda r: (r % 4) * 64 + r // 4)
    perms[3] = one_hot(lambda r: (r % 32) * 8 + r // 32)

    def project(u, source):
        gain = gains_ref[u, 0:1, :]
        for p in range(4):
            row, half = p // 2, p % 2
            lanes = slice(half * 256, half * 256 + 256)
            zf = source[row, lanes, :].astype(F32)
            centred = zf - jnp.mean(zf, axis=1, keepdims=True)
            variance = jnp.mean(centred * centred, axis=1, keepdims=True)
            nb = (centred * lax.rsqrt(variance + 1e-05) * gain).astype(BF)
            normed[u, row, lanes, :] = nb
            mask = mask_ref[row : row + 1, lanes].astype(F32)
            for lr in range(2):
                proj = dot(wt[u, lr * 256 : lr * 256 + 256, :], nb, 1, 1)
                edge = jax.nn.sigmoid(proj[:128]) * proj[128:] * mask
                edges[lr, :, p * 256 : p * 256 + 256] = edge.astype(BF)
        for b in range(8):
            rows = slice(b * 16, b * 16 + 16)
            stack = jnp.concatenate(
                [edges[lr, rows, j * 128 : j * 128 + 128] for lr in range(2) for j in range(8)], axis=0
            )
            tiles = dot(perms[0], stack, 1, 0).astype(BF)
            send1[u, rows] = tiles.reshape(16, 16, 128)

    def scatter_edges(u):
        def one(i, carry):
            k = i // 16
            tz = (2 * zhi + zlo + far_first(k, 8)) % 8
            tx = (x + far_first(i % 4, 4)) % 4
            ty = (y + far_first((i // 4) % 4, 4)) % 4
            tl, tg = tz % 2, tz // 2
            h = ((tl * 4 + ty) * 4 + tx) * 4 + tg
            own = (h == channel) & (zlo == core)

            @pl.when(jnp.logical_not(own))
            def _():
                pltpu.make_async_remote_copy(
                    src_ref=send1.at[u, h], dst_ref=recv1.at[u, slot], send_sem=s1.at[u], recv_sem=r1.at[u],
                    device_id=device(tx, ty, tl, tg, zlo), device_id_type=MESH,
                ).start()

            @pl.when(own)
            def _():
                pltpu.make_async_copy(send1.at[u, h], recv1.at[u, slot], r1.at[u]).start()

            return carry

        lax.fori_loop(0, 128, one, 0)

    def scatter_products(u):
        def one(i, carry):
            tx, ty, tg, tc = partner(i)
            at = ((ty * 4 + tx) * 2 + tc) * 4 + tg
            own = (at == slot) & (zlo == core)

            @pl.when(jnp.logical_not(own))
            def _():
                pltpu.make_async_remote_copy(
                    src_ref=send2.at[u, at], dst_ref=recv2.at[u, channel], send_sem=s2.at[u], recv_sem=r2.at[u],
                    device_id=device(tx, ty, core, tg, tc), device_id_type=MESH,
                ).start()

            @pl.when(own)
            def _():
                pltpu.make_async_copy(send2.at[u, at], recv2.at[u, channel], r2.at[u]).start()

            return carry

        lax.fori_loop(0, 128, one, 0)

    def wait_all(buf, sem):
        pltpu.make_async_copy(buf, buf, sem).wait()

    def to_sibling(src, dst, i):
        copy = pltpu.make_async_remote_copy(
            src_ref=src, dst_ref=dst, send_sem=sx.at[i], recv_sem=rx.at[i], device_id=sibling, device_id_type=MESH
        )
        copy.start()
        return copy

    def multiply(u):
        wait_all(recv1.at[u], r1.at[u])
        for b in range(8):
            block = recv1[u, b * 16 : b * 16 + 16].reshape(256, 128)
            sorted_ = dot(perms[1], block, 1, 0).astype(BF)
            rows = slice(b * 32, b * 32 + 32)
            for k in range(4):
                lanes = slice(k * 128, k * 128 + 128)
                right[u, core, rows, lanes] = sorted_[128 + k * 32 : 160 + k * 32]
                if u == 0:
                    left[k // 2, rows, (k % 2) * 128 : (k % 2) * 128 + 128] = sorted_[k * 32 : k * 32 + 32]
                else:
                    left[2 + k // 2, rows, (k % 2) * 128 : (k % 2) * 128 + 128] = sorted_[k * 32 : k * 32 + 32]
        copies = [to_sibling(right.at[u, core], right.at[u, core], u)]
        if u == 1:
            copies.append(to_sibling(left.at[2 + 1 - core], leftx, 2))
        if u == 0:
            for step in range(2):
                if step == 1:
                    copies[0].wait_recv()
                half = core if step == 0 else 1 - core
                rhs = right[u, half]
                total = dot(left[0], rhs[:, :256], 1, 1) + dot(left[1], rhs[:, 256:], 1, 1)
                prod[half] = total.astype(BF)
        else:
            mine = left[2 + core]
            totals = [dot(mine, right[u, core, :, j * 256 : j * 256 + 256], 0, 0) for j in range(2)]
            for copy in copies:
                copy.wait_recv()
            for j in range(2):
                other = dot(leftx[...], right[u, 1 - core, :, j * 256 : j * 256 + 256], 0, 0)
                prod[j] = (totals[j] + other).astype(BF)
        for b in range(4):
            rows = slice(b * 64, b * 64 + 64)
            stack = jnp.concatenate(
                [prod[j // 2, rows, (j % 2) * 128 : (j % 2) * 128 + 128] for j in range(4)], axis=0
            )
            tiles = dot(perms[2], stack, 1, 0).reshape(32, 8, 128)
            send2[u, b * 32 : b * 32 + 32] = tiles.astype(BF)
        return copies

    def finish(u, source, target):
        wait_all(recv2.at[u], r2.at[u])
        for b in range(4):
            block = recv2[u, b * 32 : b * 32 + 32].astype(F32).reshape(256, 128).astype(BF)
            tiles = dot(perms[3], block, 1, 0).astype(BF)
            for j in range(8):
                chan[b * 32 : b * 32 + 32, j * 128 : j * 128 + 128] = tiles[j * 32 : j * 32 + 32]
        gain = gains_ref[u, 1:2, :].reshape(128, 1)
        for p in range(4):
            row, half = p // 2, p % 2
            lanes = slice(half * 256, half * 256 + 256)
            values = chan[:, p * 256 : p * 256 + 256].astype(F32)
            centred = values - jnp.mean(values, axis=0, keepdims=True)
            variance = jnp.mean(centred * centred, axis=0, keepdims=True)
            scaled = (centred * lax.rsqrt(variance + 1e-05) * gain).astype(BF)
            projected = dot(scaled, wo_ref[u], 0, 0)
            gating = jax.nn.sigmoid(dot(normed[u, row, lanes, :], wg_ref[u], 1, 0))
            result = source[row, lanes, :].astype(F32) + gating * projected
            target[row, lanes, :] = result.astype(BF)

    copies = []
    for u in range(2):
        source, target = (z_ref, cur) if u == 0 else (cur, out_ref)
        project(u, source)
        if u == 0:
            pl.semaphore_wait(barrier, 128)
        scatter_edges(u)
        copies += multiply(u)
        scatter_products(u)
        finish(u, source, target)

    for copy in copies:
        copy.wait_send()
    for u in range(2):

        @pl.when(zlo == core)
        def _():
            wait_all(send1.at[u, pl.ds(0, 127)], s1.at[u])
            wait_all(send2.at[u, pl.ds(0, 127)], s2.at[u])

        @pl.when(zlo != core)
        def _():
            wait_all(send1.at[u], s1.at[u])
            wait_all(send2.at[u], s2.at[u])


def per_device(pair_map, pair_mask, edge_weights, gate_weights, out_weights, norm_gains):
    vmem = pl.BlockSpec(memory_space=pltpu.VMEM)
    return pl.pallas_call(
        kernel,
        out_shape=jax.ShapeDtypeStruct((2, 512, 128), BF),
        in_specs=[vmem] * 6,
        out_specs=vmem,
        scratch_shapes=[
            pltpu.VMEM((2, 512, 128), BF),
            pltpu.VMEM((4, 256, 256), BF),
            pltpu.VMEM((2, 2, 512, 128), BF),
            pltpu.VMEM((2, 512, 128), BF),
            pltpu.VMEM((2, 128, 1024), BF),
            pltpu.VMEM((2, 128, 16, 128), BF),
            pltpu.VMEM((2, 128, 16, 128), BF),
            pltpu.VMEM((4, 256, 256), BF),
            pltpu.VMEM((2, 2, 256, 512), BF),
            pltpu.VMEM((256, 256), BF),
            pltpu.VMEM((2, 256, 256), BF),
            pltpu.VMEM((2, 128, 8, 128), BF),
            pltpu.VMEM((2, 128, 8, 128), BF),
            pltpu.VMEM((128, 1024), BF),
            pltpu.SemaphoreType.DMA((2,)),
            pltpu.SemaphoreType.DMA((2,)),
            pltpu.SemaphoreType.DMA((2,)),
            pltpu.SemaphoreType.DMA((2,)),
            pltpu.SemaphoreType.DMA((3,)),
            pltpu.SemaphoreType.DMA((3,)),
        ],
        compiler_params=pltpu.CompilerParams(
            collective_id=0, has_side_effects=True, vmem_limit_bytes=40 * 1024 * 1024
        ),
        name="triangles",
    )(pair_map, pair_mask, edge_weights, gate_weights, out_weights, norm_gains)


def solution(mesh):
    return jax.shard_map(
        per_device,
        mesh=mesh,
        in_specs=(P(("dap", "grp"), None, None), P(("dap", "grp"), None), P(), P(), P(), P()),
        out_specs=P(("dap", "grp"), None, None),
        check_vma=False,
    )
```

time: 181 us -> 91.5 us (0.51)
  Pallas kernels: 0 us -> 85.5 us
  waiting for transfers between devices: 82.6 us -> 0 us
  blocking collectives: 33.9 us -> 0 us
  starting transfers between devices: 26.2 us -> 0 us
  between operations: 13.7 us -> 0.02 us
  local copies, waits for them, and re-layouts: 13.7 us -> 5.65 us
  other arithmetic: 5.97 us -> 0 us
  matrix products: 4.57 us -> 0 us
    pallas_call x0 -> x1, Pallas kernels: none -> 85.5 us  [per_device(): pl.pallas_call(kernel, out_shape=jax.ShapeDtypeStruct((2, 512, 128), BF),...]
    all_to_all x4 -> x0, waiting for transfers between devices: 35.8 us -> none  [the longest x2 17.9 us: finish(): lax.all_to_all(product_map.astype(jnp.bfloat16), 'dap', split_axis=0, con...]
    all_to_all x2 -> x0, blocking collectives: 33.9 us -> none  [the longest x1 19.9 us: edge_maps(): lax.all_to_all(right_edges, 'dap', split_axis=0, concat_axis=1, tiled=True)]
    unnamed x3 -> x0, waiting for transfers between devices: 28.3 us -> none
    all_to_all x4 -> x0, starting transfers between devices: 26.1 us -> none  [the longest x2 17.1 us: finish(): lax.all_to_all(product_map.astype(jnp.bfloat16), 'dap', split_axis=0, con...]
    all_gather x1 -> x0, waiting for transfers between devices: 18.6 us -> none  [per_device(): gathered = lax.all_gather(right_edges, 'grp', axis=1, tiled=True)]
    dot_general x10 -> x0, matrix products: 4.57 us -> none  [the longest x2 1.41 us: finish(): jnp.einsum('rhn,hc->rnc', scaled, out_weights[layer_idx], preferred_eleme...]
    reduce_sum x7 -> x0, other arithmetic: 4.11 us -> none  [the longest x4 2.45 us: normalize(): variance = jnp.mean(centred * centred, axis=axis, keepdims=True)]
  transfers between devices with their start and end apart: 6 -> 0, of which waited for: 6 -> 0; matrix products, arithmetic and copies ran while one was open for 2% -> 0% of each run, Pallas kernels for 0% -> 0%
where the time goes in v1:
time: 91.5 us; the launch traced here: 91.2 us
  Pallas kernels  85.5 us (93%)
  local copies, waits for them, and re-layouts  5.65 us (6%)
    pallas_call x1, Pallas kernels, per_device(): pl.pallas_call(kernel, out_shape=jax.ShapeDtypeStruct((2, 512, 128), BF),...  85.5 us
    unnamed x13, local copies, waits for them, and re-layouts  5.65 us

profile of v1, /device:TPU:1, one launch (start us, length us, event | category | flops | bytes accessed | tf_op | source)
XLA Modules:
  0.0 91.2 jit_solution(16679413719935954069)
XLA Ops:
  0.0 0.0 copy-start
  0.0 0.9 %copy-done = bf16[2,512,128]{2,1,0:T(8,128)(2,1)S(1)} copy-done((bf16[2,512,128]{2,1,0:T(8,128)(2,1)S(1)}, bf16[2,512,128]{2,1,0:T(8,128)(2,1)}, u32[]{:S(2)}) %copy-start) | copy-done | bytes 262168
  1.0 0.0 copy-start.1
  1.0 0.9 %copy-done.1 = bf16[2,128,512]{2,1,0:T(8,128)(2,1)S(1)} copy-done((bf16[2,128,512]{2,1,0:T(8,128)(2,1)S(1)}, bf16[2,128,512]{2,1,0:T(8,128)(2,1)}, u32[]{:S(2)}) %copy-start.1) | copy-done | bytes 262168
  1.9 0.0 copy-start.2
  1.9 0.8 copy-done.2
  2.7 0.0 copy-start.3
  2.7 0.8 copy-done.3
  3.6 0.0 copy-start.4
  3.6 0.7 copy-done.4
  4.3 0.0 copy-start.5
  4.3 0.7 copy-done.5
  5.0 85.5 %triangles.1 = bf16[2,512,128]{2,1,0:T(8,128)(2,1)S(1)} custom-call(bf16[2,512,128]{2,1,0:T(8,128)(2,1)S(1)} %copy-done, s32[2,512]{1,0:T(2,128)S(1)} %copy-done.4, bf16[2,128,512]{2,1,0:T(8,128)(2,1)S(1)} %copy-done.1, bf16[2,128,128]{2,1,0:T(8,128)(2,1)S(1)} %copy-done.2, bf16[2,128,128]{2,1,0:T(8,128)(2,1)S(1)} %copy-done.3, f32[2,2,128]{2,1,0:T(2,128)S(1)} %copy-done.5), custom_call_target="tpu_custom_call" | custom-call | tf_op jit(solution)/shard_map/triangles/pallas_call | solution.py:247
  90.5 0.7 copy.8
Async XLA Ops:
  0.0 0.9 %copy-start = (bf16[2,512,128]{2,1,0:T(8,128)(2,1)S(1)}, bf16[2,512,128]{2,1,0:T(8,128)(2,1)}, u32[]{:S(2)}) copy-start(bf16[2,512,128]{2,1,0:T(8,128)(2,1)} %z_ref.1) | copy-start | bytes 786436
  1.0 0.9 %copy-start.1 = (bf16[2,128,512]{2,1,0:T(8,128)(2,1)S(1)}, bf16[2,128,512]{2,1,0:T(8,128)(2,1)}, u32[]{:S(2)}) copy-start(bf16[2,128,512]{2,1,0:T(8,128)(2,1)} %we_ref.1) | copy-start | bytes 786436
  1.9 0.8 copy-start.2
  2.7 0.8 copy-start.3
  3.6 0.7 copy-start.4
  4.3 0.7 copy-start.5

commit v2 on v1

--- a/solution.py
+++ b/solution.py
@@ -36,26 +36,57 @@
     return (((zlo * 4 + y) * 4 + x) * 2 + core, zhi)
 
 
-def far_first(k, size):
-    return (size // 2 + jnp.where(k % 2 == 1, size - (k + 1) // 2, k // 2)) % size
-
-
-def kernel(z_ref, mask_ref, we_ref, wg_ref, wo_ref, gains_ref, out_ref,
-           wt, perms, normed, cur, edges, send1, recv1, left, right, leftx, prod, send2, recv2, chan,
-           s1, r1, s2, r2, sx, rx):
+XY = sorted(range(16), key=lambda o: (-(2 - abs(o % 4 - 2)) - (2 - abs(o // 4 - 2)), o))
+XY_WORDS = [sum(o << (4 * i) for i, o in enumerate(XY[w : w + 7])) for w in (0, 7, 14)]
+
+
+def xy_offset(i):
+    word = jnp.where(i < 7, XY_WORDS[0], jnp.where(i < 14, XY_WORDS[1], XY_WORDS[2]))
+    o = (word >> (4 * (i % 7))) % 16
+    return o % 4, o // 4
+
+
+def all_offset(i):
+    j = i - 16
+    ends = (j < 0) | (j >= 96)
+    far = 3 - j // 32
+    dz = jnp.where(j < 0, 4, jnp.where(j >= 96, 0, jnp.where(j % 2 == 1, 8 - far, far)))
+    dx, dy = xy_offset(jnp.where(ends, i % 16, (j % 32) // 2))
+    return dx, dy, dz
+
+
+def half_offset(i, odd):
+    m = jnp.where(odd, i, i - 16)
+    single = jnp.logical_not(odd) & ((m < 0) | (m >= 32))
+    far = jnp.where(odd, 3 - 2 * (i // 32), jnp.where(m < 0, 4, jnp.where(m >= 32, 0, 2)))
+    dz = jnp.where(jnp.logical_not(single) & (i % 2 == 1), 8 - far, far)
+    dx, dy = xy_offset(jnp.where(single, i % 16, (m % 32) // 2))
+    return dx, dy, dz
+
+
+def kernel(z_hbm, mask_hbm, we_hbm, wg_hbm, wo_hbm, gains_hbm, out_ref,
+           z_ref, mask_ref, we_ref, wg_ref, wo_ref, gains_ref, wt, perms, normed, cur, edges, send1, recv1, left, right, leftx, prod, send2, recv2, chan,
+           s1, r1, s2, r2, sx, rx, load):
     x, y, zlo, zhi, core = where_am_i()
     slot = ((y * 4 + x) * 2 + core) * 4 + zhi
     channel = ((zlo * 4 + y) * 4 + x) * 4 + zhi
     sibling = device(x, y, zlo, zhi, 1 - core)
 
+    loads = [
+        pltpu.make_async_copy(src, dst, load.at[i])
+        for i, (src, dst) in enumerate(
+            ((z_hbm, z_ref), (we_hbm, we_ref), (gains_hbm, gains_ref), (mask_hbm, mask_ref),
+             (wg_hbm, wg_ref), (wo_hbm, wo_ref))
+        )
+    ]
+    for copy in loads:
+        copy.start()
+
     barrier = pltpu.get_barrier_semaphore()
 
     def partner(i):
-        tc, k = i % 2, i // 2
-        tg = (zhi + far_first(k // 16, 4)) % 4
-        tx = (x + far_first(k % 4, 4)) % 4
-        ty = (y + far_first((k // 4) % 4, 4)) % 4
-        return tx, ty, tg, tc
+        dx, dy, dz = half_offset(i % 64, zlo != core)
+        return (x + dx) % 4, (y + dy) % 4, ((2 * zhi + zlo + dz) % 8) // 2, i // 64
 
     def greet(i, carry):
         tx, ty, tg, tc = partner(i)
@@ -69,12 +100,15 @@
     pl.semaphore_signal(barrier, inc=1, device_id=sibling, device_id_type=MESH)
     lax.fori_loop(0, 128, greet, 0)
 
-    for u in range(2):
-        wt[u] = we_ref[u].astype(F32).T.astype(BF)
     perms[0] = one_hot(lambda r: (r % 16) * 16 + r // 16)
     perms[1] = one_hot(lambda r: ((r // 2) % 16) * 16 + (r // 128) * 8 + (r % 2) * 4 + (r // 32) % 4)
     perms[2] = one_hot(lambda r: (r % 4) * 64 + r // 4)
     perms[3] = one_hot(lambda r: (r % 32) * 8 + r // 32)
+
+    for copy in loads:
+        copy.wait()
+    for u in range(2):
+        wt[u] = we_ref[u].astype(F32).T.astype(BF)
 
     def project(u, source):
         gain = gains_ref[u, 0:1, :]
@@ -101,10 +135,8 @@
 
     def scatter_edges(u):
         def one(i, carry):
-            k = i // 16
-            tz = (2 * zhi + zlo + far_first(k, 8)) % 8
-            tx = (x + far_first(i % 4, 4)) % 4
-            ty = (y + far_first((i // 4) % 4, 4)) % 4
+            dx, dy, dz = all_offset(i)
+            tx, ty, tz = (x + dx) % 4, (y + dy) % 4, (2 * zhi + zlo + dz) % 8
             tl, tg = tz % 2, tz // 2
             h = ((tl * 4 + ty) * 4 + tx) * 4 + tg
             own = (h == channel) & (zlo == core)
@@ -247,9 +279,15 @@
     return pl.pallas_call(
         kernel,
         out_shape=jax.ShapeDtypeStruct((2, 512, 128), BF),
-        in_specs=[vmem] * 6,
+        in_specs=[pl.BlockSpec(memory_space=pl.ANY)] * 6,
         out_specs=vmem,
         scratch_shapes=[
+            pltpu.VMEM((2, 512, 128), BF),
+            pltpu.VMEM((2, 512), jnp.int32),
+            pltpu.VMEM((2, 128, 512), BF),
+            pltpu.VMEM((2, 128, 128), BF),
+            pltpu.VMEM((2, 128, 128), BF),
+            pltpu.VMEM((2, 2, 128), F32),
             pltpu.VMEM((2, 512, 128), BF),
             pltpu.VMEM((4, 256, 256), BF),
             pltpu.VMEM((2, 2, 512, 128), BF),
@@ -270,6 +308,7 @@
             pltpu.SemaphoreType.DMA((2,)),
             pltpu.SemaphoreType.DMA((3,)),
             pltpu.SemaphoreType.DMA((3,)),
+            pltpu.SemaphoreType.DMA((6,)),
         ],
         compiler_params=pltpu.CompilerParams(
             collective_id=0, has_side_effects=True, vmem_limit_bytes=40 * 1024 * 1024

time: 91.5 us -> 85.5 us (0.934)
  Pallas kernels: 85.5 us -> 79.6 us
    pallas_call x1, Pallas kernels: 85.5 us -> 79.6 us  [per_device(): pl.pallas_call(kernel, out_shape=jax.ShapeDtypeStruct((2, 512, 128), BF),...]
where the time goes in v2:
time: 85.5 us; the launch traced here: 85.3 us
  Pallas kernels  79.6 us (93%)
  local copies, waits for them, and re-layouts  5.65 us (7%)
    pallas_call x1, Pallas kernels, per_device(): pl.pallas_call(kernel, out_shape=jax.ShapeDtypeStruct((2, 512, 128), BF),...  79.6 us
    unnamed x13, local copies, waits for them, and re-layouts  5.65 us

profile of v2, /device:TPU:1, one launch (start us, length us, event | category | flops | bytes accessed | tf_op | source)
XLA Modules:
  0.0 85.3 jit_solution(14427533615931510184)
XLA Ops:
  0.0 0.0 copy-start
  0.0 0.9 %copy-done = bf16[2,512,128]{2,1,0:T(8,128)(2,1)S(1)} copy-done((bf16[2,512,128]{2,1,0:T(8,128)(2,1)S(1)}, bf16[2,512,128]{2,1,0:T(8,128)(2,1)}, u32[]{:S(2)}) %copy-start) | copy-done | bytes 262168
  1.0 0.0 copy-start.1
  1.0 0.9 %copy-done.1 = bf16[2,128,512]{2,1,0:T(8,128)(2,1)S(1)} copy-done((bf16[2,128,512]{2,1,0:T(8,128)(2,1)S(1)}, bf16[2,128,512]{2,1,0:T(8,128)(2,1)}, u32[]{:S(2)}) %copy-start.1) | copy-done | bytes 262168
  1.9 0.0 copy-start.2
  1.9 0.8 copy-done.2
  2.7 0.0 copy-start.3
  2.7 0.8 copy-done.3
  3.6 0.0 copy-start.4
  3.6 0.7 copy-done.4
  4.3 0.0 copy-start.5
  4.3 0.7 copy-done.5
  5.0 79.6 %triangles.1 = bf16[2,512,128]{2,1,0:T(8,128)(2,1)S(1)} custom-call(bf16[2,512,128]{2,1,0:T(8,128)(2,1)S(1)} %copy-done, s32[2,512]{1,0:T(2,128)S(1)} %copy-done.4, bf16[2,128,512]{2,1,0:T(8,128)(2,1)S(1)} %copy-done.1, bf16[2,128,128]{2,1,0:T(8,128)(2,1)S(1)} %copy-done.2, bf16[2,128,128]{2,1,0:T(8,128)(2,1)S(1)} %copy-done.3, f32[2,2,128]{2,1,0:T(2,128)S(1)} %copy-done.5), custom_call_target="tpu_custom_call" | custom-call | tf_op jit(solution)/shard_map/triangles/pallas_call | solution.py:279
  84.6 0.7 copy.8
Async XLA Ops:
  0.0 0.9 %copy-start = (bf16[2,512,128]{2,1,0:T(8,128)(2,1)S(1)}, bf16[2,512,128]{2,1,0:T(8,128)(2,1)}, u32[]{:S(2)}) copy-start(bf16[2,512,128]{2,1,0:T(8,128)(2,1)} %z_hbm.1) | copy-start | bytes 786436
  1.0 0.9 %copy-start.1 = (bf16[2,128,512]{2,1,0:T(8,128)(2,1)S(1)}, bf16[2,128,512]{2,1,0:T(8,128)(2,1)}, u32[]{:S(2)}) copy-start(bf16[2,128,512]{2,1,0:T(8,128)(2,1)} %we_hbm.1) | copy-start | bytes 786436
  1.9 0.8 copy-start.2
  2.7 0.8 copy-start.3
  3.6 0.7 copy-start.4
  4.3 0.7 copy-start.5

commit v3 on v2

--- a/solution.py
+++ b/solution.py
@@ -22,55 +22,38 @@
     return jnp.where(cols == source(rows), 1.0, 0.0).astype(BF)
 
 
-def where_am_i():
-    dap = lax.axis_index("dap")
-    grp = lax.axis_index("grp")
-    core = dap % 2
-    x = (dap // 2) % 4
-    y = (dap // 8) % 4
-    zlo = dap // 32
-    return x, y, zlo, grp, core
-
-
-def device(x, y, zlo, zhi, core):
-    return (((zlo * 4 + y) * 4 + x) * 2 + core, zhi)
-
-
-XY = sorted(range(16), key=lambda o: (-(2 - abs(o % 4 - 2)) - (2 - abs(o // 4 - 2)), o))
-XY_WORDS = [sum(o << (4 * i) for i, o in enumerate(XY[w : w + 7])) for w in (0, 7, 14)]
-
-
-def xy_offset(i):
-    word = jnp.where(i < 7, XY_WORDS[0], jnp.where(i < 14, XY_WORDS[1], XY_WORDS[2]))
-    o = (word >> (4 * (i % 7))) % 16
-    return o % 4, o // 4
-
-
-def all_offset(i):
-    j = i - 16
-    ends = (j < 0) | (j >= 96)
-    far = 3 - j // 32
-    dz = jnp.where(j < 0, 4, jnp.where(j >= 96, 0, jnp.where(j % 2 == 1, 8 - far, far)))
-    dx, dy = xy_offset(jnp.where(ends, i % 16, (j % 32) // 2))
-    return dx, dy, dz
-
-
-def half_offset(i, odd):
-    m = jnp.where(odd, i, i - 16)
-    single = jnp.logical_not(odd) & ((m < 0) | (m >= 32))
-    far = jnp.where(odd, 3 - 2 * (i // 32), jnp.where(m < 0, 4, jnp.where(m >= 32, 0, 2)))
-    dz = jnp.where(jnp.logical_not(single) & (i % 2 == 1), 8 - far, far)
-    dx, dy = xy_offset(jnp.where(single, i % 16, (m % 32) // 2))
-    return dx, dy, dz
+def ring(mask):
+    return (0, 1, 2, 1)[mask]
+
+
+XY_MASKS = sorted(((x, y) for x in range(4) for y in range(4)), key=lambda m: -ring(m[0]) - ring(m[1]))
+Z_MASKS = (4, 5, 7, 3, 2, 6, 1, 0)
+Z_EVEN = (4, 2, 6, 0)
+Z_ODD = (5, 7, 3, 1)
+
+
+def packed(masks):
+    return sum((((m & 1) << 3) | (m >> 1)) << (4 * i) for i, m in enumerate(masks) if i < 7)
+
+
+def nibble(word, i):
+    return (word >> (4 * i)) & 15
+
+
+def mesh_id(number):
+    return (number >> 2, number & 3)
 
 
 def kernel(z_hbm, mask_hbm, we_hbm, wg_hbm, wo_hbm, gains_hbm, out_ref,
            z_ref, mask_ref, we_ref, wg_ref, wo_ref, gains_ref, wt, perms, normed, cur, edges, send1, recv1, left, right, leftx, prod, send2, recv2, chan,
            s1, r1, s2, r2, sx, rx, load):
-    x, y, zlo, zhi, core = where_am_i()
-    slot = ((y * 4 + x) * 2 + core) * 4 + zhi
-    channel = ((zlo * 4 + y) * 4 + x) * 4 + zhi
-    sibling = device(x, y, zlo, zhi, 1 - core)
+    dap = lax.axis_index("dap")
+    number = dap * 4 + lax.axis_index("grp")
+    core = (number >> 2) & 1
+    zlo = number >> 7
+    slot = number & 127
+    channel = ((number >> 3) << 2) | (number & 3)
+    sibling = mesh_id(number ^ 4)
 
     loads = [
         pltpu.make_async_copy(src, dst, load.at[i])
@@ -84,21 +67,26 @@
 
     barrier = pltpu.get_barrier_semaphore()
 
-    def partner(i):
-        dx, dy, dz = half_offset(i % 64, zlo != core)
-        return (x + dx) % 4, (y + dy) % 4, ((2 * zhi + zlo + dz) % 8) // 2, i // 64
-
-    def greet(i, carry):
-        tx, ty, tg, tc = partner(i)
-
-        @pl.when(jnp.logical_not((tx == x) & (ty == y) & (tg == zhi) & (zlo == core)))
+    def partners(visit):
+        word = jnp.where(zlo == core, packed(Z_EVEN), packed(Z_ODD))
+        chip = number - core * 4
+
+        def one(k, carry):
+            z = nibble(word, k & 3)
+            base = chip ^ (((z >> 3) << 7) | (z & 3) | ((k >> 2) << 2))
+            for mx, my in XY_MASKS:
+                visit(base ^ (my << 5 | mx << 3))
+            return carry
+
+        lax.fori_loop(0, 8, one, 0)
+
+    def greet(other):
+        @pl.when((other | 4) != (number | 4))
         def _():
-            pl.semaphore_signal(barrier, inc=1, device_id=device(tx, ty, core, tg, tc), device_id_type=MESH)
-
-        return carry
+            pl.semaphore_signal(barrier, inc=1, device_id=mesh_id(other), device_id_type=MESH)
 
     pl.semaphore_signal(barrier, inc=1, device_id=sibling, device_id_type=MESH)
-    lax.fori_loop(0, 128, greet, 0)
+    partners(greet)
 
     perms[0] = one_hot(lambda r: (r % 16) * 16 + r // 16)
     perms[1] = one_hot(lambda r: ((r // 2) % 16) * 16 + (r // 128) * 8 + (r % 2) * 4 + (r // 32) % 4)
@@ -134,48 +122,46 @@
             send1[u, rows] = tiles.reshape(16, 16, 128)
 
     def scatter_edges(u):
-        def one(i, carry):
-            dx, dy, dz = all_offset(i)
-            tx, ty, tz = (x + dx) % 4, (y + dy) % 4, (2 * zhi + zlo + dz) % 8
-            tl, tg = tz % 2, tz // 2
-            h = ((tl * 4 + ty) * 4 + tx) * 4 + tg
-            own = (h == channel) & (zlo == core)
-
-            @pl.when(jnp.logical_not(own))
-            def _():
-                pltpu.make_async_remote_copy(
+        base = (number - core * 4) | (zlo << 2)
+
+        def one(k, carry):
+            z = jnp.where(k == 7, 0, nibble(packed(Z_MASKS), k))
+            for mx, my in XY_MASKS:
+                other = base ^ (((z >> 3) << 7) | (z & 3) | (my << 5 | mx << 3))
+                h = channel ^ (((z >> 3) << 6) | (z & 3) | (my << 4 | mx << 2))
+                copy = pltpu.make_async_remote_copy(
                     src_ref=send1.at[u, h], dst_ref=recv1.at[u, slot], send_sem=s1.at[u], recv_sem=r1.at[u],
-                    device_id=device(tx, ty, tl, tg, zlo), device_id_type=MESH,
-                ).start()
-
-            @pl.when(own)
-            def _():
-                pltpu.make_async_copy(send1.at[u, h], recv1.at[u, slot], r1.at[u]).start()
+                    device_id=mesh_id(other), device_id_type=MESH,
+                )
+                if mx or my:
+                    copy.start()
+                    continue
+                pl.when(other != number)(copy.start)
+
+                @pl.when(other == number)
+                def _():
+                    pltpu.make_async_copy(send1.at[u, h], recv1.at[u, slot], r1.at[u]).start()
 
             return carry
 
-        lax.fori_loop(0, 128, one, 0)
+        lax.fori_loop(0, 8, one, 0)
 
     def scatter_products(u):
-        def one(i, carry):
-            tx, ty, tg, tc = partner(i)
-            at = ((ty * 4 + tx) * 2 + tc) * 4 + tg
-            own = (at == slot) & (zlo == core)
-
-            @pl.when(jnp.logical_not(own))
+        def send(other):
+            at = other & 127
+
+            @pl.when(other != number)
             def _():
                 pltpu.make_async_remote_copy(
                     src_ref=send2.at[u, at], dst_ref=recv2.at[u, channel], send_sem=s2.at[u], recv_sem=r2.at[u],
-                    device_id=device(tx, ty, core, tg, tc), device_id_type=MESH,
+                    device_id=mesh_id(other), device_id_type=MESH,
                 ).start()
 
-            @pl.when(own)
+            @pl.when(other == number)
             def _():
                 pltpu.make_async_copy(send2.at[u, at], recv2.at[u, channel], r2.at[u]).start()
 
-            return carry
-
-        lax.fori_loop(0, 128, one, 0)
+        partners(send)
 
     def wait_all(buf, sem):
         pltpu.make_async_copy(buf, buf, sem).wait()

time: 85.5 us -> 76.4 us (0.89)
  Pallas kernels: 79.6 us -> 70.4 us
    pallas_call x1, Pallas kernels: 79.6 us -> 70.4 us  [per_device(): pl.pallas_call(kernel, out_shape=jax.ShapeDtypeStruct((2, 512, 128), BF),...]
where the time goes in v3:
time: 76.4 us; the launch traced here: 76.1 us
  Pallas kernels  70.4 us (92%)
  local copies, waits for them, and re-layouts  5.65 us (7%)
    pallas_call x1, Pallas kernels, per_device(): pl.pallas_call(kernel, out_shape=jax.ShapeDtypeStruct((2, 512, 128), BF),...  70.4 us
    unnamed x13, local copies, waits for them, and re-layouts  5.65 us

profile of v3, /device:TPU:1, one launch (start us, length us, event | category | flops | bytes accessed | tf_op | source)
XLA Modules:
  0.0 76.1 jit_solution(2478935073723483453)
XLA Ops:
  0.0 0.0 copy-start
  0.0 0.9 %copy-done = bf16[2,512,128]{2,1,0:T(8,128)(2,1)S(1)} copy-done((bf16[2,512,128]{2,1,0:T(8,128)(2,1)S(1)}, bf16[2,512,128]{2,1,0:T(8,128)(2,1)}, u32[]{:S(2)}) %copy-start) | copy-done | bytes 262168
  1.0 0.0 copy-start.1
  1.0 0.9 %copy-done.1 = bf16[2,128,512]{2,1,0:T(8,128)(2,1)S(1)} copy-done((bf16[2,128,512]{2,1,0:T(8,128)(2,1)S(1)}, bf16[2,128,512]{2,1,0:T(8,128)(2,1)}, u32[]{:S(2)}) %copy-start.1) | copy-done | bytes 262168
  1.9 0.0 copy-start.2
  1.9 0.8 %copy-done.2 = bf16[2,128,128]{2,1,0:T(8,128)(2,1)S(1)} copy-done((bf16[2,128,128]{2,1,0:T(8,128)(2,1)S(1)}, bf16[2,128,128]{2,1,0:T(8,128)(2,1)}, u32[]{:S(2)}) %copy-start.2) | copy-done | bytes 65560
  2.7 0.0 copy-start.3
  2.7 0.8 %copy-done.3 = bf16[2,128,128]{2,1,0:T(8,128)(2,1)S(1)} copy-done((bf16[2,128,128]{2,1,0:T(8,128)(2,1)S(1)}, bf16[2,128,128]{2,1,0:T(8,128)(2,1)}, u32[]{:S(2)}) %copy-start.3) | copy-done | bytes 65560
  3.6 0.0 copy-start.4
  3.6 0.7 copy-done.4
  4.3 0.0 copy-start.5
  4.3 0.7 copy-done.5
  5.0 70.4 %triangles.1 = bf16[2,512,128]{2,1,0:T(8,128)(2,1)S(1)} custom-call(bf16[2,512,128]{2,1,0:T(8,128)(2,1)S(1)} %copy-done, s32[2,512]{1,0:T(2,128)S(1)} %copy-done.4, bf16[2,128,512]{2,1,0:T(8,128)(2,1)S(1)} %copy-done.1, bf16[2,128,128]{2,1,0:T(8,128)(2,1)S(1)} %copy-done.2, bf16[2,128,128]{2,1,0:T(8,128)(2,1)S(1)} %copy-done.3, f32[2,2,128]{2,1,0:T(2,128)S(1)} %copy-done.5), custom_call_target="tpu_custom_call" | custom-call | tf_op jit(solution)/shard_map/triangles/pallas_call | solution.py:265
  75.4 0.7 copy.8
Async XLA Ops:
  0.0 0.9 %copy-start = (bf16[2,512,128]{2,1,0:T(8,128)(2,1)S(1)}, bf16[2,512,128]{2,1,0:T(8,128)(2,1)}, u32[]{:S(2)}) copy-start(bf16[2,512,128]{2,1,0:T(8,128)(2,1)} %z_hbm.1) | copy-start | bytes 786436
  1.0 0.9 %copy-start.1 = (bf16[2,128,512]{2,1,0:T(8,128)(2,1)S(1)}, bf16[2,128,512]{2,1,0:T(8,128)(2,1)}, u32[]{:S(2)}) copy-start(bf16[2,128,512]{2,1,0:T(8,128)(2,1)} %we_hbm.1) | copy-start | bytes 786436
  1.9 0.8 %copy-start.2 = (bf16[2,128,128]{2,1,0:T(8,128)(2,1)S(1)}, bf16[2,128,128]{2,1,0:T(8,128)(2,1)}, u32[]{:S(2)}) copy-start(bf16[2,128,128]{2,1,0:T(8,128)(2,1)} %wg_hbm.1) | copy-start | bytes 196612
  2.7 0.8 %copy-start.3 = (bf16[2,128,128]{2,1,0:T(8,128)(2,1)S(1)}, bf16[2,128,128]{2,1,0:T(8,128)(2,1)}, u32[]{:S(2)}) copy-start(bf16[2,128,128]{2,1,0:T(8,128)(2,1)} %wo_hbm.1) | copy-start | bytes 196612
  3.6 0.7 copy-start.4
  4.3 0.7 copy-start.5

commit v4 on v3

--- a/solution.py
+++ b/solution.py
@@ -88,8 +88,8 @@
     pl.semaphore_signal(barrier, inc=1, device_id=sibling, device_id_type=MESH)
     partners(greet)
 
-    perms[0] = one_hot(lambda r: (r % 16) * 16 + r // 16)
-    perms[1] = one_hot(lambda r: ((r // 2) % 16) * 16 + (r // 128) * 8 + (r % 2) * 4 + (r // 32) % 4)
+    perms[0] = one_hot(lambda r: (r % 8) * 32 + r // 8)
+    perms[1] = one_hot(lambda r: ((r // 2) % 32) * 8 + (r % 2) * 4 + r // 64)
     perms[2] = one_hot(lambda r: (r % 4) * 64 + r // 4)
     perms[3] = one_hot(lambda r: (r % 32) * 8 + r // 32)
 
@@ -98,30 +98,28 @@
     for u in range(2):
         wt[u] = we_ref[u].astype(F32).T.astype(BF)
 
-    def project(u, source):
+    def normalize_rows(u, source):
         gain = gains_ref[u, 0:1, :]
         for p in range(4):
-            row, half = p // 2, p % 2
-            lanes = slice(half * 256, half * 256 + 256)
+            row, lanes = p // 2, slice(p % 2 * 256, p % 2 * 256 + 256)
             zf = source[row, lanes, :].astype(F32)
             centred = zf - jnp.mean(zf, axis=1, keepdims=True)
             variance = jnp.mean(centred * centred, axis=1, keepdims=True)
-            nb = (centred * lax.rsqrt(variance + 1e-05) * gain).astype(BF)
-            normed[u, row, lanes, :] = nb
+            normed[u, row, lanes, :] = (centred * lax.rsqrt(variance + 1e-05) * gain).astype(BF)
+
+    def project(u, lr):
+        for p in range(4):
+            row, lanes = p // 2, slice(p % 2 * 256, p % 2 * 256 + 256)
             mask = mask_ref[row : row + 1, lanes].astype(F32)
-            for lr in range(2):
-                proj = dot(wt[u, lr * 256 : lr * 256 + 256, :], nb, 1, 1)
-                edge = jax.nn.sigmoid(proj[:128]) * proj[128:] * mask
-                edges[lr, :, p * 256 : p * 256 + 256] = edge.astype(BF)
-        for b in range(8):
-            rows = slice(b * 16, b * 16 + 16)
-            stack = jnp.concatenate(
-                [edges[lr, rows, j * 128 : j * 128 + 128] for lr in range(2) for j in range(8)], axis=0
-            )
-            tiles = dot(perms[0], stack, 1, 0).astype(BF)
-            send1[u, rows] = tiles.reshape(16, 16, 128)
-
-    def scatter_edges(u):
+            proj = dot(wt[u, lr * 256 : lr * 256 + 256, :], normed[u, row, lanes, :], 1, 1)
+            edge = jax.nn.sigmoid(proj[:128]) * proj[128:] * mask
+            edges[lr, :, p * 256 : p * 256 + 256] = edge.astype(BF)
+        for b in range(4):
+            rows = slice(b * 32, b * 32 + 32)
+            stack = jnp.concatenate([edges[lr, rows, j * 128 : j * 128 + 128] for j in range(8)], axis=0)
+            send1[u, lr, rows] = dot(perms[0], stack, 1, 0).reshape(32, 8, 128).astype(BF)
+
+    def scatter_edges(u, lr):
         base = (number - core * 4) | (zlo << 2)
 
         def one(k, carry):
@@ -130,7 +128,8 @@
                 other = base ^ (((z >> 3) << 7) | (z & 3) | (my << 5 | mx << 3))
                 h = channel ^ (((z >> 3) << 6) | (z & 3) | (my << 4 | mx << 2))
                 copy = pltpu.make_async_remote_copy(
-                    src_ref=send1.at[u, h], dst_ref=recv1.at[u, slot], send_sem=s1.at[u], recv_sem=r1.at[u],
+                    src_ref=send1.at[u, lr, h], dst_ref=recv1.at[u, lr, slot], send_sem=s1.at[u, lr],
+                    recv_sem=r1.at[u, lr],
                     device_id=mesh_id(other), device_id_type=MESH,
                 )
                 if mx or my:
@@ -140,7 +139,7 @@
 
                 @pl.when(other == number)
                 def _():
-                    pltpu.make_async_copy(send1.at[u, h], recv1.at[u, slot], r1.at[u]).start()
+                    pltpu.make_async_copy(send1.at[u, lr, h], recv1.at[u, lr, slot], r1.at[u, lr]).start()
 
             return carry
 
@@ -173,20 +172,21 @@
         copy.start()
         return copy
 
+    def gathered(u, lr, b):
+        wanted = recv1[u, lr, b * 32 : b * 32 + 32].astype(F32).reshape(256, 128).astype(BF)
+        blocks = dot(perms[1], wanted, 1, 0).astype(BF)
+        return [blocks[k * 64 : k * 64 + 64] for k in range(4)]
+
     def multiply(u):
-        wait_all(recv1.at[u], r1.at[u])
-        for b in range(8):
-            block = recv1[u, b * 16 : b * 16 + 16].reshape(256, 128)
-            sorted_ = dot(perms[1], block, 1, 0).astype(BF)
-            rows = slice(b * 32, b * 32 + 32)
-            for k in range(4):
-                lanes = slice(k * 128, k * 128 + 128)
-                right[u, core, rows, lanes] = sorted_[128 + k * 32 : 160 + k * 32]
-                if u == 0:
-                    left[k // 2, rows, (k % 2) * 128 : (k % 2) * 128 + 128] = sorted_[k * 32 : k * 32 + 32]
-                else:
-                    left[2 + k // 2, rows, (k % 2) * 128 : (k % 2) * 128 + 128] = sorted_[k * 32 : k * 32 + 32]
+        wait_all(recv1.at[u, 1], r1.at[u, 1])
+        for b in range(4):
+            for k, block in enumerate(gathered(u, 1, b)):
+                right[u, core, b * 64 : b * 64 + 64, k * 128 : k * 128 + 128] = block
         copies = [to_sibling(right.at[u, core], right.at[u, core], u)]
+        wait_all(recv1.at[u, 0], r1.at[u, 0])
+        for b in range(4):
+            for k, block in enumerate(gathered(u, 0, b)):
+                left[2 * u + k // 2, b * 64 : b * 64 + 64, k % 2 * 128 : k % 2 * 128 + 128] = block
         if u == 1:
             copies.append(to_sibling(left.at[2 + 1 - core], leftx, 2))
         if u == 0:
@@ -237,10 +237,18 @@
     copies = []
     for u in range(2):
         source, target = (z_ref, cur) if u == 0 else (cur, out_ref)
-        project(u, source)
+        normalize_rows(u, source)
         if u == 0:
+            project(u, 1)
+            project(u, 0)
             pl.semaphore_wait(barrier, 128)
-        scatter_edges(u)
+            scatter_edges(u, 1)
+            scatter_edges(u, 0)
+        else:
+            project(u, 1)
+            scatter_edges(u, 1)
+            project(u, 0)
+            scatter_edges(u, 0)
         copies += multiply(u)
         scatter_products(u)
         finish(u, source, target)
@@ -251,12 +259,14 @@
 
         @pl.when(zlo == core)
         def _():
-            wait_all(send1.at[u, pl.ds(0, 127)], s1.at[u])
+            for lr in range(2):
+                wait_all(send1.at[u, lr, pl.ds(0, 127)], s1.at[u, lr])
             wait_all(send2.at[u, pl.ds(0, 127)], s2.at[u])
 
         @pl.when(zlo != core)
         def _():
-            wait_all(send1.at[u], s1.at[u])
+            for lr in range(2):
+                wait_all(send1.at[u, lr], s1.at[u, lr])
             wait_all(send2.at[u], s2.at[u])
 
 
@@ -279,8 +289,8 @@
             pltpu.VMEM((2, 2, 512, 128), BF),
             pltpu.VMEM((2, 512, 128), BF),
             pltpu.VMEM((2, 128, 1024), BF),
-            pltpu.VMEM((2, 128, 16, 128), BF),
-            pltpu.VMEM((2, 128, 16, 128), BF),
+            pltpu.VMEM((2, 2, 128, 8, 128), BF),
+            pltpu.VMEM((2, 2, 128, 8, 128), BF),
             pltpu.VMEM((4, 256, 256), BF),
             pltpu.VMEM((2, 2, 256, 512), BF),
             pltpu.VMEM((256, 256), BF),
@@ -288,8 +298,8 @@
             pltpu.VMEM((2, 128, 8, 128), BF),
             pltpu.VMEM((2, 128, 8, 128), BF),
             pltpu.VMEM((128, 1024), BF),
-            pltpu.SemaphoreType.DMA((2,)),
-            pltpu.SemaphoreType.DMA((2,)),
+            pltpu.SemaphoreType.DMA((2, 2)),
+            pltpu.SemaphoreType.DMA((2, 2)),
             pltpu.SemaphoreType.DMA((2,)),
             pltpu.SemaphoreType.DMA((2,)),
             pltpu.SemaphoreType.DMA((3,)),

time: 76.4 us -> 75.1 us (0.983)
  Pallas kernels: 70.4 us -> 69.1 us
    pallas_call x1, Pallas kernels: 70.4 us -> 69.1 us  [per_device(): pl.pallas_call(kernel, out_shape=jax.ShapeDtypeStruct((2, 512, 128), BF),...]
where the time goes in v4:
time: 75.1 us; the launch traced here: 74.8 us
  Pallas kernels  69.1 us (92%)
  local copies, waits for them, and re-layouts  5.65 us (8%)
    pallas_call x1, Pallas kernels, per_device(): pl.pallas_call(kernel, out_shape=jax.ShapeDtypeStruct((2, 512, 128), BF),...  69.1 us
    unnamed x13, local copies, waits for them, and re-layouts  5.65 us

profile of v4, /device:TPU:1, one launch (start us, length us, event | category | flops | bytes accessed | tf_op | source)
XLA Modules:
  0.0 74.8 jit_solution(6411160787157274321)
XLA Ops:
  0.0 0.0 copy-start
  0.0 0.9 %copy-done = bf16[2,512,128]{2,1,0:T(8,128)(2,1)S(1)} copy-done((bf16[2,512,128]{2,1,0:T(8,128)(2,1)S(1)}, bf16[2,512,128]{2,1,0:T(8,128)(2,1)}, u32[]{:S(2)}) %copy-start) | copy-done | bytes 262168
  1.0 0.0 copy-start.1
  1.0 0.9 %copy-done.1 = bf16[2,128,512]{2,1,0:T(8,128)(2,1)S(1)} copy-done((bf16[2,128,512]{2,1,0:T(8,128)(2,1)S(1)}, bf16[2,128,512]{2,1,0:T(8,128)(2,1)}, u32[]{:S(2)}) %copy-start.1) | copy-done | bytes 262168
  1.9 0.0 copy-start.2
  1.9 0.8 %copy-done.2 = bf16[2,128,128]{2,1,0:T(8,128)(2,1)S(1)} copy-done((bf16[2,128,128]{2,1,0:T(8,128)(2,1)S(1)}, bf16[2,128,128]{2,1,0:T(8,128)(2,1)}, u32[]{:S(2)}) %copy-start.2) | copy-done | bytes 65560
  2.7 0.0 copy-start.3
  2.7 0.8 %copy-done.3 = bf16[2,128,128]{2,1,0:T(8,128)(2,1)S(1)} copy-done((bf16[2,128,128]{2,1,0:T(8,128)(2,1)S(1)}, bf16[2,128,128]{2,1,0:T(8,128)(2,1)}, u32[]{:S(2)}) %copy-start.3) | copy-done | bytes 65560
  3.6 0.0 copy-start.4
  3.6 0.7 copy-done.4
  4.3 0.0 copy-start.5
  4.3 0.7 copy-done.5
  5.0 69.1 %triangles.1 = bf16[2,512,128]{2,1,0:T(8,128)(2,1)S(1)} custom-call(bf16[2,512,128]{2,1,0:T(8,128)(2,1)S(1)} %copy-done, s32[2,512]{1,0:T(2,128)S(1)} %copy-done.4, bf16[2,128,512]{2,1,0:T(8,128)(2,1)S(1)} %copy-done.1, bf16[2,128,128]{2,1,0:T(8,128)(2,1)S(1)} %copy-done.2, bf16[2,128,128]{2,1,0:T(8,128)(2,1)S(1)} %copy-done.3, f32[2,2,128]{2,1,0:T(2,128)S(1)} %copy-done.5), custom_call_target="tpu_custom_call" | custom-call | tf_op jit(solution)/shard_map/triangles/pallas_call | solution.py:275
  74.1 0.7 copy.8
Async XLA Ops:
  0.0 0.9 %copy-start = (bf16[2,512,128]{2,1,0:T(8,128)(2,1)S(1)}, bf16[2,512,128]{2,1,0:T(8,128)(2,1)}, u32[]{:S(2)}) copy-start(bf16[2,512,128]{2,1,0:T(8,128)(2,1)} %z_hbm.1) | copy-start | bytes 786436
  1.0 0.9 %copy-start.1 = (bf16[2,128,512]{2,1,0:T(8,128)(2,1)S(1)}, bf16[2,128,512]{2,1,0:T(8,128)(2,1)}, u32[]{:S(2)}) copy-start(bf16[2,128,512]{2,1,0:T(8,128)(2,1)} %we_hbm.1) | copy-start | bytes 786436
  1.9 0.8 %copy-start.2 = (bf16[2,128,128]{2,1,0:T(8,128)(2,1)S(1)}, bf16[2,128,128]{2,1,0:T(8,128)(2,1)}, u32[]{:S(2)}) copy-start(bf16[2,128,128]{2,1,0:T(8,128)(2,1)} %wg_hbm.1) | copy-start | bytes 196612
  2.7 0.8 %copy-start.3 = (bf16[2,128,128]{2,1,0:T(8,128)(2,1)S(1)}, bf16[2,128,128]{2,1,0:T(8,128)(2,1)}, u32[]{:S(2)}) copy-start(bf16[2,128,128]{2,1,0:T(8,128)(2,1)} %wo_hbm.1) | copy-start | bytes 196612
  3.6 0.7 copy-start.4
  4.3 0.7 copy-start.5

commit v5 on v4

v5 whole, which is shorter than its diff:
```python
import functools

import jax
import jax.numpy as jnp
from jax import lax
from jax.experimental import pallas as pl
from jax.experimental.pallas import tpu as pltpu
from jax.sharding import PartitionSpec as P

BF = jnp.bfloat16
F32 = jnp.float32
MESH = pl.DeviceIdType.MESH


def dot(a, b, ca, cb):
    return lax.dot_general(a, b, (((ca,), (cb,)), ((), ())), preferred_element_type=F32)


def one_hot(source):
    rows = lax.broadcasted_iota(jnp.int32, (256, 256), 0)
    cols = lax.broadcasted_iota(jnp.int32, (256, 256), 1)
    return jnp.where(cols == source(rows), 1.0, 0.0).astype(BF)


def ring(mask):
    return (0, 1, 2, 1)[mask]


XY_MASKS = sorted(((x, y) for x in range(4) for y in range(4)), key=lambda m: -ring(m[0]) - ring(m[1]))
Z_MASKS = (4, 5, 7, 3, 2, 6, 1, 0)
Z_EVEN = (4, 2, 6, 0)
Z_ODD = (5, 7, 3, 1)


def packed(masks):
    return sum((((m & 1) << 3) | (m >> 1)) << (4 * i) for i, m in enumerate(masks) if i < 7)


def nibble(word, i):
    return (word >> (4 * i)) & 15


def mesh_id(number):
    return (number >> 2, number & 3)


def kernel(z_hbm, mask_hbm, we_hbm, wg_hbm, wo_hbm, gains_hbm, out_ref,
           z_ref, mask_ref, we_ref, wg_ref, wo_ref, gains_ref, wt, perms, normed, cur, edges, send1, recv1, left, right, prod, send2, recv2,
           send3, recv3, pairs, send4, recv4, chan, s1, r1, s2, r2, s3, r3, s4, r4, sx, rx, load):
    dap = lax.axis_index("dap")
    number = dap * 4 + lax.axis_index("grp")
    core = (number >> 2) & 1
    zlo = number >> 7
    slot = number & 127
    channel = ((number >> 3) << 2) | (number & 3)
    sibling = mesh_id(number ^ 4)

    loads = [
        pltpu.make_async_copy(src, dst, load.at[i])
        for i, (src, dst) in enumerate(
            ((z_hbm, z_ref), (we_hbm, we_ref), (gains_hbm, gains_ref), (mask_hbm, mask_ref),
             (wg_hbm, wg_ref), (wo_hbm, wo_ref))
        )
    ]
    for copy in loads:
        copy.start()

    barrier = pltpu.get_barrier_semaphore()

    def partners(visit):
        word = jnp.where(zlo == core, packed(Z_EVEN), packed(Z_ODD))
        chip = number - core * 4

        def one(k, carry):
            z = nibble(word, k & 3)
            base = chip ^ (((z >> 3) << 7) | (z & 3) | ((k >> 2) << 2))
            for mx, my in XY_MASKS:
                visit(base ^ (my << 5 | mx << 3))
            return carry

        lax.fori_loop(0, 8, one, 0)

    def greet(other):
        @pl.when((other | 4) != (number | 4))
        def _():
            pl.semaphore_signal(barrier, inc=1, device_id=mesh_id(other), device_id_type=MESH)

    pl.semaphore_signal(barrier, inc=1, device_id=sibling, device_id_type=MESH)
    partners(greet)

    perms[0] = one_hot(lambda r: (r % 8) * 32 + r // 8)
    perms[1] = one_hot(lambda r: ((r // 2) % 32) * 8 + (r % 2) * 4 + r // 64)
    perms[4] = one_hot(lambda r: (r % 16) * 16 + r // 16)
    perms[5] = one_hot(lambda r: ((r // 2) % 16) * 16 + (r // 128) * 8 + (r % 2) * 4 + (r // 32) % 4)
    perms[2] = one_hot(lambda r: (r % 4) * 64 + r // 4)
    perms[3] = one_hot(lambda r: (r % 32) * 8 + r // 32)

    for copy in loads:
        copy.wait()
    for u in range(2):
        wt[u] = we_ref[u].astype(F32).T.astype(BF)

    def normalize_rows(u, source):
        gain = gains_ref[u, 0:1, :]
        for p in range(4):
            row, lanes = p // 2, slice(p % 2 * 256, p % 2 * 256 + 256)
            zf = source[row, lanes, :].astype(F32)
            centred = zf - jnp.mean(zf, axis=1, keepdims=True)
            variance = jnp.mean(centred * centred, axis=1, keepdims=True)
            normed[u, row, lanes, :] = (centred * lax.rsqrt(variance + 1e-05) * gain).astype(BF)

    def edge_map(u, lr):
        for p in range(4):
            row, lanes = p // 2, slice(p % 2 * 256, p % 2 * 256 + 256)
            mask = mask_ref[row : row + 1, lanes].astype(F32)
            proj = dot(wt[u, lr * 256 : lr * 256 + 256, :], normed[u, row, lanes, :], 1, 1)
            edge = jax.nn.sigmoid(proj[:128]) * proj[128:] * mask
            edges[lr, :, p * 256 : p * 256 + 256] = edge.astype(BF)

    def pack_one(lr):
        for b in range(4):
            rows = slice(b * 32, b * 32 + 32)
            stack = jnp.concatenate([edges[lr, rows, j * 128 : j * 128 + 128] for j in range(8)], axis=0)
            send1[lr, rows] = dot(perms[0], stack, 1, 0).reshape(32, 8, 128).astype(BF)

    def pack_both():
        for b in range(8):
            rows = slice(b * 16, b * 16 + 16)
            stack = jnp.concatenate(
                [edges[lr, rows, j * 128 : j * 128 + 128] for lr in range(2) for j in range(8)], axis=0
            )
            send3[rows] = dot(perms[4], stack, 1, 0).astype(BF).reshape(16, 16, 128)

    def scatter_edges(lr):
        base = (number - core * 4) | (zlo << 2)

        def one(k, carry):
            z = jnp.where(k == 7, 0, nibble(packed(Z_MASKS), k))
            for mx, my in XY_MASKS:
                other = base ^ (((z >> 3) << 7) | (z & 3) | (my << 5 | mx << 3))
                h = channel ^ (((z >> 3) << 6) | (z & 3) | (my << 4 | mx << 2))
                copy = pltpu.make_async_remote_copy(
                    src_ref=send1.at[lr, h], dst_ref=recv1.at[lr, slot], send_sem=s1.at[lr],
                    recv_sem=r1.at[lr],
                    device_id=mesh_id(other), device_id_type=MESH,
                )
                if mx or my:
                    copy.start()
                    continue
                pl.when(other != number)(copy.start)

                @pl.when(other == number)
                def _():
                    pltpu.make_async_copy(send1.at[lr, h], recv1.at[lr, slot], r1.at[lr]).start()

            return carry

        lax.fori_loop(0, 8, one, 0)

    def scatter_products():
        def send(other):
            at = other & 127

            @pl.when(other != number)
            def _():
                pltpu.make_async_remote_copy(
                    src_ref=send2.at[at], dst_ref=recv2.at[channel], send_sem=s2, recv_sem=r2,
                    device_id=mesh_id(other), device_id_type=MESH,
                ).start()

            @pl.when(other == number)
            def _():
                pltpu.make_async_copy(send2.at[at], recv2.at[channel], r2).start()

        partners(send)

    mine = ((number >> 2) << 1) | (number & 1)

    def scatter_pairs():
        z = ((number & 3) << 1) | zlo
        plane = number & (15 << 3)

        def one(k, carry):
            worker_core = k & 1
            step = k >> 1
            dz = jnp.where(step == 0, 2 + 4 * worker_core, jnp.where(step == 1, 1, jnp.where(step == 2, 7, 0)))
            wz = (z + dz) & 7
            base = ((wz & 1) << 7) | plane | (worker_core << 2) | (wz >> 1)
            for mx, my in XY_MASKS:
                other = base ^ (my << 5 | mx << 3)
                h = ((other >> 2) << 1) | (other & 1)
                copy = pltpu.make_async_remote_copy(
                    src_ref=send3.at[h], dst_ref=recv3.at[mine], send_sem=s3, recv_sem=r3,
                    device_id=mesh_id(other), device_id_type=MESH,
                )
                if mx or my:
                    copy.start()
                    continue
                pl.when(other != number)(copy.start)

                @pl.when(other == number)
                def _():
                    pltpu.make_async_copy(send3.at[h], recv3.at[mine], r3).start()

            return carry

        lax.fori_loop(0, 8, one, 0)

    def scatter_parts():
        part = (number >> 1) & 1

        def one(k, carry):
            zk = k >> 1
            z = jnp.where(zk == 7, 0, nibble(packed(Z_MASKS), zk))
            base = number ^ (((z >> 3) << 7) | (z & 3) | ((k & 1) << 2))
            for mx, my in XY_MASKS:
                other = base ^ (my << 5 | mx << 3)
                copy = pltpu.make_async_remote_copy(
                    src_ref=send4.at[other], dst_ref=recv4.at[part, mine], send_sem=s4, recv_sem=r4,
                    device_id=mesh_id(other), device_id_type=MESH,
                )
                if mx or my:
                    copy.start()
                    continue
                pl.when(other != number)(copy.start)

                @pl.when(other == number)
                def _():
                    pltpu.make_async_copy(send4.at[other], recv4.at[part, mine], r4).start()

            return carry

        lax.fori_loop(0, 16, one, 0)

    def wait_all(buf, sem):
        pltpu.make_async_copy(buf, buf, sem).wait()

    def gathered(lr, b):
        wanted = recv1[lr, b * 32 : b * 32 + 32].astype(F32).reshape(256, 128).astype(BF)
        blocks = dot(perms[1], wanted, 1, 0).astype(BF)
        return [blocks[k * 64 : k * 64 + 64] for k in range(4)]

    def messages(rows_of):
        stack = jnp.concatenate(rows_of, axis=0)
        return dot(perms[2], stack, 1, 0).reshape(32, 8, 128).astype(BF)

    def multiply_outgoing():
        wait_all(recv1.at[1], r1.at[1])
        for b in range(4):
            for k, block in enumerate(gathered(1, b)):
                right[core, b * 64 : b * 64 + 64, k * 128 : k * 128 + 128] = block
        relay = pltpu.make_async_remote_copy(
            src_ref=right.at[core], dst_ref=right.at[core], send_sem=sx, recv_sem=rx, device_id=sibling,
            device_id_type=MESH,
        )
        relay.start()
        wait_all(recv1.at[0], r1.at[0])
        for b in range(4):
            for k, block in enumerate(gathered(0, b)):
                left[b * 64 : b * 64 + 64, k * 128 : k * 128 + 128] = block
        for step in range(2):
            if step == 1:
                relay.wait_recv()
            half = core if step == 0 else 1 - core
            prod[half] = dot(left[...], right[half], 1, 1).astype(BF)
        for b in range(4):
            rows = slice(b * 64, b * 64 + 64)
            send2[b * 32 : b * 32 + 32] = messages(
                [prod[j // 2, rows, (j % 2) * 128 : (j % 2) * 128 + 128] for j in range(4)]
            )
        return relay

    def multiply_incoming():
        wait_all(recv3, r3)
        for b in range(8):
            wanted = recv3[b * 16 : b * 16 + 16].reshape(256, 128)
            blocks = dot(perms[5], wanted, 1, 0).astype(BF)
            for lr in range(2):
                for k in range(4):
                    pairs[lr, b * 32 : b * 32 + 32, k * 128 : k * 128 + 128] = blocks[
                        lr * 128 + k * 32 : lr * 128 + k * 32 + 32
                    ]
        for i in range(2):
            part = dot(pairs[0, :, i * 256 : i * 256 + 256], pairs[1], 0, 0).astype(BF)
            for b in range(4):
                send4[i * 128 + b * 32 : i * 128 + b * 32 + 32] = messages(
                    [part[b * 64 : b * 64 + 64, j * 128 : j * 128 + 128] for j in range(4)]
                )

    def by_channel(buf, b):
        block = buf[b * 32 : b * 32 + 32].astype(F32).reshape(256, 128).astype(BF)
        return dot(perms[3], block, 1, 0)

    def finish(u, source, target):
        if u == 0:
            wait_all(recv2, r2)
        else:
            wait_all(recv4, r4)
        for b in range(4):
            if u == 0:
                tiles = by_channel(recv2, b)
            else:
                tiles = by_channel(recv4.at[0], b) + by_channel(recv4.at[1], b)
            for j in range(8):
                chan[b * 32 : b * 32 + 32, j * 128 : j * 128 + 128] = tiles[j * 32 : j * 32 + 32]
        gain = gains_ref[u, 1:2, :].reshape(128, 1)
        for p in range(4):
            row, half = p // 2, p % 2
            lanes = slice(half * 256, half * 256 + 256)
            values = chan[:, p * 256 : p * 256 + 256]
            centred = values - jnp.mean(values, axis=0, keepdims=True)
            variance = jnp.mean(centred * centred, axis=0, keepdims=True)
            scaled = (centred * lax.rsqrt(variance + 1e-05) * gain).astype(BF)
            projected = dot(scaled, wo_ref[u], 0, 0)
            gating = jax.nn.sigmoid(dot(normed[u, row, lanes, :], wg_ref[u], 1, 0))
            result = source[row, lanes, :].astype(F32) + gating * projected
            target[row, lanes, :] = result.astype(BF)

    normalize_rows(0, z_ref)
    for lr in (1, 0):
        edge_map(0, lr)
        pack_one(lr)
    pl.semaphore_wait(barrier, 128)
    scatter_edges(1)
    scatter_edges(0)
    relay = multiply_outgoing()
    scatter_products()
    finish(0, z_ref, cur)

    normalize_rows(1, cur)
    edge_map(1, 0)
    edge_map(1, 1)
    pack_both()
    scatter_pairs()
    multiply_incoming()
    scatter_parts()
    finish(1, cur, out_ref)

    relay.wait_send()
    wait_all(send3.at[pl.ds(0, 127)], s3)
    wait_all(send4.at[pl.ds(0, 255)], s4)

    @pl.when(zlo == core)
    def _():
        for lr in range(2):
            wait_all(send1.at[lr, pl.ds(0, 127)], s1.at[lr])
        wait_all(send2.at[pl.ds(0, 127)], s2)

    @pl.when(zlo != core)
    def _():
        for lr in range(2):
            wait_all(send1.at[lr], s1.at[lr])
        wait_all(send2, s2)


def per_device(pair_map, pair_mask, edge_weights, gate_weights, out_weights, norm_gains):
    vmem = pl.BlockSpec(memory_space=pltpu.VMEM)
    return pl.pallas_call(
        kernel,
        out_shape=jax.ShapeDtypeStruct((2, 512, 128), BF),
        in_specs=[pl.BlockSpec(memory_space=pl.ANY)] * 6,
        out_specs=vmem,
        scratch_shapes=[
            pltpu.VMEM((2, 512, 128), BF),
            pltpu.VMEM((2, 512), jnp.int32),
            pltpu.VMEM((2, 128, 512), BF),
            pltpu.VMEM((2, 128, 128), BF),
            pltpu.VMEM((2, 128, 128), BF),
            pltpu.VMEM((2, 2, 128), F32),
            pltpu.VMEM((2, 512, 128), BF),
            pltpu.VMEM((6, 256, 256), BF),
            pltpu.VMEM((2, 2, 512, 128), BF),
            pltpu.VMEM((2, 512, 128), BF),
            pltpu.VMEM((2, 128, 1024), BF),
            pltpu.VMEM((2, 128, 8, 128), BF),
            pltpu.VMEM((2, 128, 8, 128), BF),
            pltpu.VMEM((256, 512), BF),
            pltpu.VMEM((2, 256, 512), BF),
            pltpu.VMEM((2, 256, 256), BF),
            pltpu.VMEM((128, 8, 128), BF),
            pltpu.VMEM((128, 8, 128), BF),
            pltpu.VMEM((128, 16, 128), BF),
            pltpu.VMEM((128, 16, 128), BF),
            pltpu.VMEM((2, 256, 512), BF),
            pltpu.VMEM((256, 8, 128), BF),
            pltpu.VMEM((2, 128, 8, 128), BF),
            pltpu.VMEM((128, 1024), F32),
            pltpu.SemaphoreType.DMA((2,)),
            pltpu.SemaphoreType.DMA((2,)),
        ]
        + [pltpu.SemaphoreType.DMA] * 8
        + [
            pltpu.SemaphoreType.DMA((6,)),
        ],
        compiler_params=pltpu.CompilerParams(
            collective_id=0, has_side_effects=True, vmem_limit_bytes=40 * 1024 * 1024
        ),
        name="triangles",
    )(pair_map, pair_mask, edge_weights, gate_weights, out_weights, norm_gains)


def solution(mesh):
    return jax.shard_map(
        per_device,
        mesh=mesh,
        in_specs=(P(("dap", "grp"), None, None), P(("dap", "grp"), None), P(), P(), P(), P()),
        out_specs=P(("dap", "grp"), None, None),
        check_vma=False,
    )
```

time: 75.1 us -> 73.6 us (0.980)
  Pallas kernels: 69.1 us -> 67.6 us
    pallas_call x1, Pallas kernels: 69.1 us -> 67.6 us  [per_device(): pl.pallas_call(kernel, out_shape=jax.ShapeDtypeStruct((2, 512, 128), BF),...]
where the time goes in v5:
time: 73.6 us; the launch traced here: 73.3 us
  Pallas kernels  67.6 us (92%)
  local copies, waits for them, and re-layouts  5.65 us (8%)
    pallas_call x1, Pallas kernels, per_device(): pl.pallas_call(kernel, out_shape=jax.ShapeDtypeStruct((2, 512, 128), BF),...  67.6 us
    unnamed x13, local copies, waits for them, and re-layouts  5.65 us

profile of v5, /device:TPU:1, one launch (start us, length us, event | category | flops | bytes accessed | tf_op | source)
XLA Modules:
  0.0 73.3 jit_solution(6875811422576183836)
XLA Ops:
  0.0 0.0 copy-start
  0.0 0.9 %copy-done = bf16[2,512,128]{2,1,0:T(8,128)(2,1)S(1)} copy-done((bf16[2,512,128]{2,1,0:T(8,128)(2,1)S(1)}, bf16[2,512,128]{2,1,0:T(8,128)(2,1)}, u32[]{:S(2)}) %copy-start) | copy-done | bytes 262168
  1.0 0.0 copy-start.1
  1.0 0.9 %copy-done.1 = bf16[2,128,512]{2,1,0:T(8,128)(2,1)S(1)} copy-done((bf16[2,128,512]{2,1,0:T(8,128)(2,1)S(1)}, bf16[2,128,512]{2,1,0:T(8,128)(2,1)}, u32[]{:S(2)}) %copy-start.1) | copy-done | bytes 262168
  1.9 0.0 copy-start.2
  1.9 0.8 %copy-done.2 = bf16[2,128,128]{2,1,0:T(8,128)(2,1)S(1)} copy-done((bf16[2,128,128]{2,1,0:T(8,128)(2,1)S(1)}, bf16[2,128,128]{2,1,0:T(8,128)(2,1)}, u32[]{:S(2)}) %copy-start.2) | copy-done | bytes 65560
  2.7 0.0 copy-start.3
  2.7 0.8 %copy-done.3 = bf16[2,128,128]{2,1,0:T(8,128)(2,1)S(1)} copy-done((bf16[2,128,128]{2,1,0:T(8,128)(2,1)S(1)}, bf16[2,128,128]{2,1,0:T(8,128)(2,1)}, u32[]{:S(2)}) %copy-start.3) | copy-done | bytes 65560
  3.6 0.0 copy-start.4
  3.6 0.7 copy-done.4
  4.3 0.0 copy-start.5
  4.3 0.7 copy-done.5
  5.0 67.6 %triangles.1 = bf16[2,512,128]{2,1,0:T(8,128)(2,1)S(1)} custom-call(bf16[2,512,128]{2,1,0:T(8,128)(2,1)S(1)} %copy-done, s32[2,512]{1,0:T(2,128)S(1)} %copy-done.4, bf16[2,128,512]{2,1,0:T(8,128)(2,1)S(1)} %copy-done.1, bf16[2,128,128]{2,1,0:T(8,128)(2,1)S(1)} %copy-done.2, bf16[2,128,128]{2,1,0:T(8,128)(2,1)S(1)} %copy-done.3, f32[2,2,128]{2,1,0:T(2,128)S(1)} %copy-done.5), custom_call_target="tpu_custom_call" | custom-call | tf_op jit(solution)/shard_map/triangles/pallas_call | solution.py:358
  72.6 0.7 copy.8
Async XLA Ops:
  0.0 0.9 %copy-start = (bf16[2,512,128]{2,1,0:T(8,128)(2,1)S(1)}, bf16[2,512,128]{2,1,0:T(8,128)(2,1)}, u32[]{:S(2)}) copy-start(bf16[2,512,128]{2,1,0:T(8,128)(2,1)} %z_hbm.1) | copy-start | bytes 786436
  1.0 0.9 %copy-start.1 = (bf16[2,128,512]{2,1,0:T(8,128)(2,1)S(1)}, bf16[2,128,512]{2,1,0:T(8,128)(2,1)}, u32[]{:S(2)}) copy-start(bf16[2,128,512]{2,1,0:T(8,128)(2,1)} %we_hbm.1) | copy-start | bytes 786436
  1.9 0.8 %copy-start.2 = (bf16[2,128,128]{2,1,0:T(8,128)(2,1)S(1)}, bf16[2,128,128]{2,1,0:T(8,128)(2,1)}, u32[]{:S(2)}) copy-start(bf16[2,128,128]{2,1,0:T(8,128)(2,1)} %wg_hbm.1) | copy-start | bytes 196612
  2.7 0.8 %copy-start.3 = (bf16[2,128,128]{2,1,0:T(8,128)(2,1)S(1)}, bf16[2,128,128]{2,1,0:T(8,128)(2,1)}, u32[]{:S(2)}) copy-start(bf16[2,128,128]{2,1,0:T(8,128)(2,1)} %wo_hbm.1) | copy-start | bytes 196612
  3.6 0.7 copy-start.4
  4.3 0.7 copy-start.5

commit v6 on v5

v6 whole, which is shorter than its diff:
```python
import functools

import jax
import jax.numpy as jnp
from jax import lax
from jax.experimental import pallas as pl
from jax.experimental.pallas import tpu as pltpu
from jax.sharding import PartitionSpec as P

BF = jnp.bfloat16
F32 = jnp.float32
MESH = pl.DeviceIdType.MESH


def dot(a, b, ca, cb):
    return lax.dot_general(a, b, (((ca,), (cb,)), ((), ())), preferred_element_type=F32)


def one_hot(source):
    rows = lax.broadcasted_iota(jnp.int32, (256, 256), 0)
    cols = lax.broadcasted_iota(jnp.int32, (256, 256), 1)
    return jnp.where(cols == source(rows), 1.0, 0.0).astype(BF)


def ring(mask):
    return (0, 1, 2, 1)[mask]


XY_MASKS = sorted(((x, y) for x in range(4) for y in range(4)), key=lambda m: -ring(m[0]) - ring(m[1]))


def mesh_id(number):
    return (number >> 2, number & 3)


def kernel(z_hbm, mask_hbm, we_hbm, wg_hbm, wo_hbm, gains_hbm, out_ref,
           z_ref, mask_ref, we_ref, wg_ref, wo_ref, gains_ref, wt, perms, normed, cur, edges, send1, recvl, recvr, left, right, prod, send2, recv2,
           send3, recv3, pairs, send4, recv4, chan, sl, rl, sr, rr, s2, r2, s3, r3, s4, r4, load):
    dap = lax.axis_index("dap")
    number = dap * 4 + lax.axis_index("grp")
    core = (number >> 2) & 1
    z = ((number & 3) << 1) | (number >> 7)
    plane = number & (15 << 3)
    mine = ((number >> 2) << 1) | (number & 1)

    loads = [
        pltpu.make_async_copy(src, dst, load.at[i])
        for i, (src, dst) in enumerate(
            ((z_hbm, z_ref), (we_hbm, we_ref), (gains_hbm, gains_ref), (mask_hbm, mask_ref),
             (wg_hbm, wg_ref), (wo_hbm, wo_ref))
        )
    ]
    for copy in loads:
        copy.start()

    barrier = pltpu.get_barrier_semaphore()

    def everyone(visit):
        def one(k, carry):
            i = k >> 1
            at = (z + 4 + jnp.where((i & 1) == 1, 7 - (i >> 1), i >> 1)) & 7
            base = ((at & 1) << 7) | plane | (((k & 1) ^ core) << 2) | (at >> 1)
            for mx, my in XY_MASKS:
                visit(base ^ (my << 5 | mx << 3), mx == 0 and my == 0)
            return carry

        lax.fori_loop(0, 16, one, 0)

    def neighbours(visit, workers):
        def one(k, carry):
            i = k >> 1
            far = 2 + 4 * ((k & 1) if workers else 1 - core)
            at = (z + jnp.where(i == 0, far, jnp.where(i == 1, 1, jnp.where(i == 2, 7, 0)))) & 7
            base = ((at & 1) << 7) | plane | ((k & 1) << 2) | (at >> 1)
            for mx, my in XY_MASKS:
                visit(base ^ (my << 5 | mx << 3), mx == 0 and my == 0)
            return carry

        lax.fori_loop(0, 8, one, 0)

    def short(other):
        return ((other >> 2) << 1) | (other & 1)

    def sender(place, send_sem, recv_sem):
        def send(other, maybe_self):
            src, dst = place(other)
            copy = pltpu.make_async_remote_copy(
                src_ref=src, dst_ref=dst, send_sem=send_sem, recv_sem=recv_sem, device_id=mesh_id(other),
                device_id_type=MESH,
            )
            if not maybe_self:
                copy.start()
                return
            pl.when(other != number)(copy.start)

            @pl.when(other == number)
            def _():
                pltpu.make_async_copy(src, dst, recv_sem).start()

        return send

    def greet(other, maybe_self):
        def signal():
            pl.semaphore_signal(barrier, inc=1, device_id=mesh_id(other), device_id_type=MESH)

        if maybe_self:
            pl.when(other != number)(signal)
        else:
            signal()

    everyone(greet)

    perms[0] = one_hot(lambda r: (r % 8) * 32 + r // 8)
    perms[1] = one_hot(lambda r: ((r // 2) % 32) * 8 + (r % 2) * 4 + r // 64)
    perms[4] = one_hot(lambda r: (r % 16) * 16 + r // 16)
    perms[5] = one_hot(lambda r: ((r // 2) % 16) * 16 + (r // 128) * 8 + (r % 2) * 4 + (r // 32) % 4)
    perms[2] = one_hot(lambda r: (r % 4) * 64 + r // 4)
    perms[3] = one_hot(lambda r: (r % 32) * 8 + r // 32)

    for copy in loads:
        copy.wait()
    for u in range(2):
        wt[u] = we_ref[u].astype(F32).T.astype(BF)

    def normalize_rows(u, source):
        gain = gains_ref[u, 0:1, :]
        for p in range(4):
            row, lanes = p // 2, slice(p % 2 * 256, p % 2 * 256 + 256)
            zf = source[row, lanes, :].astype(F32)
            centred = zf - jnp.mean(zf, axis=1, keepdims=True)
            variance = jnp.mean(centred * centred, axis=1, keepdims=True)
            normed[u, row, lanes, :] = (centred * lax.rsqrt(variance + 1e-05) * gain).astype(BF)

    def edge_map(u, lr):
        for p in range(4):
            row, lanes = p // 2, slice(p % 2 * 256, p % 2 * 256 + 256)
            mask = mask_ref[row : row + 1, lanes].astype(F32)
            proj = dot(wt[u, lr * 256 : lr * 256 + 256, :], normed[u, row, lanes, :], 1, 1)
            edge = jax.nn.sigmoid(proj[:128]) * proj[128:] * mask
            edges[lr, :, p * 256 : p * 256 + 256] = edge.astype(BF)

    def pack_one(lr):
        for b in range(4):
            rows = slice(b * 32, b * 32 + 32)
            stack = jnp.concatenate([edges[lr, rows, j * 128 : j * 128 + 128] for j in range(8)], axis=0)
            send1[lr, rows] = dot(perms[0], stack, 1, 0).reshape(32, 8, 128).astype(BF)

    def pack_both():
        for b in range(8):
            rows = slice(b * 16, b * 16 + 16)
            stack = jnp.concatenate(
                [edges[lr, rows, j * 128 : j * 128 + 128] for lr in range(2) for j in range(8)], axis=0
            )
            send3[rows] = dot(perms[4], stack, 1, 0).astype(BF).reshape(16, 16, 128)

    def wait_all(buf, sem):
        pltpu.make_async_copy(buf, buf, sem).wait()

    def gathered(buf, b):
        wanted = buf[b * 32 : b * 32 + 32].astype(F32).reshape(256, 128).astype(BF)
        blocks = dot(perms[1], wanted, 1, 0).astype(BF)
        return [blocks[k * 64 : k * 64 + 64] for k in range(4)]

    def messages(rows_of):
        stack = jnp.concatenate(rows_of, axis=0)
        return dot(perms[2], stack, 1, 0).reshape(32, 8, 128).astype(BF)

    def multiply_outgoing():
        for sem, buf, edge, blocks in ((rr, recvr, right, 8), (rl, recvl, left, 4)):
            wait_all(buf, sem)
            for b in range(blocks):
                for k, block in enumerate(gathered(buf, b)):
                    edge[b * 64 : b * 64 + 64, k * 128 : k * 128 + 128] = block
        for half in range(2):
            prod[half] = dot(left[...], right[half * 256 : half * 256 + 256], 1, 1).astype(BF)
        for b in range(4):
            rows = slice(b * 64, b * 64 + 64)
            send2[b * 32 : b * 32 + 32] = messages(
                [prod[j // 2, rows, (j % 2) * 128 : (j % 2) * 128 + 128] for j in range(4)]
            )

    def multiply_incoming():
        wait_all(recv3, r3)
        for b in range(8):
            wanted = recv3[b * 16 : b * 16 + 16].reshape(256, 128)
            blocks = dot(perms[5], wanted, 1, 0).astype(BF)
            for lr in range(2):
                for k in range(4):
                    pairs[lr, b * 32 : b * 32 + 32, k * 128 : k * 128 + 128] = blocks[
                        lr * 128 + k * 32 : lr * 128 + k * 32 + 32
                    ]
        for i in range(2):
            part = dot(pairs[0, :, i * 256 : i * 256 + 256], pairs[1], 0, 0).astype(BF)
            for b in range(4):
                send4[i * 128 + b * 32 : i * 128 + b * 32 + 32] = messages(
                    [part[b * 64 : b * 64 + 64, j * 128 : j * 128 + 128] for j in range(4)]
                )

    def by_channel(buf, b):
        block = buf[b * 32 : b * 32 + 32].astype(F32).reshape(256, 128).astype(BF)
        return dot(perms[3], block, 1, 0)

    def finish(u, source, target):
        if u == 0:
            wait_all(recv2, r2)
        else:
            wait_all(recv4, r4)
        for b in range(4):
            if u == 0:
                tiles = by_channel(recv2, b)
            else:
                tiles = by_channel(recv4.at[0], b) + by_channel(recv4.at[1], b)
            for j in range(8):
                chan[b * 32 : b * 32 + 32, j * 128 : j * 128 + 128] = tiles[j * 32 : j * 32 + 32]
        gain = gains_ref[u, 1:2, :].reshape(128, 1)
        for p in range(4):
            row, half = p // 2, p % 2
            lanes = slice(half * 256, half * 256 + 256)
            values = chan[:, p * 256 : p * 256 + 256]
            centred = values - jnp.mean(values, axis=0, keepdims=True)
            variance = jnp.mean(centred * centred, axis=0, keepdims=True)
            scaled = (centred * lax.rsqrt(variance + 1e-05) * gain).astype(BF)
            projected = dot(scaled, wo_ref[u], 0, 0)
            gating = jax.nn.sigmoid(dot(normed[u, row, lanes, :], wg_ref[u], 1, 0))
            result = source[row, lanes, :].astype(F32) + gating * projected
            target[row, lanes, :] = result.astype(BF)

    normalize_rows(0, z_ref)
    for lr in (1, 0):
        edge_map(0, lr)
        pack_one(lr)
    pl.semaphore_wait(barrier, 255)
    everyone(sender(lambda other: (send1.at[1, short(other)], recvr.at[number]), sr, rr))
    neighbours(sender(lambda other: (send1.at[0, short(other)], recvl.at[mine]), sl, rl), True)
    multiply_outgoing()
    neighbours(sender(lambda other: (send2.at[short(other)], recv2.at[mine]), s2, r2), False)
    finish(0, z_ref, cur)

    normalize_rows(1, cur)
    edge_map(1, 0)
    edge_map(1, 1)
    pack_both()
    neighbours(sender(lambda other: (send3.at[short(other)], recv3.at[mine]), s3, r3), True)
    multiply_incoming()
    part = (number >> 1) & 1
    everyone(sender(lambda other: (send4.at[other], recv4.at[part, mine]), s4, r4))
    finish(1, cur, out_ref)

    wait_all(send4.at[pl.ds(0, 255)], sr)
    wait_all(send1.at[0, pl.ds(0, 127)], sl)
    wait_all(send2.at[pl.ds(0, 127)], s2)
    wait_all(send3.at[pl.ds(0, 127)], s3)
    wait_all(send4.at[pl.ds(0, 255)], s4)


def per_device(pair_map, pair_mask, edge_weights, gate_weights, out_weights, norm_gains):
    vmem = pl.BlockSpec(memory_space=pltpu.VMEM)
    return pl.pallas_call(
        kernel,
        out_shape=jax.ShapeDtypeStruct((2, 512, 128), BF),
        in_specs=[pl.BlockSpec(memory_space=pl.ANY)] * 6,
        out_specs=vmem,
        scratch_shapes=[
            pltpu.VMEM((2, 512, 128), BF),
            pltpu.VMEM((2, 512), jnp.int32),
            pltpu.VMEM((2, 128, 512), BF),
            pltpu.VMEM((2, 128, 128), BF),
            pltpu.VMEM((2, 128, 128), BF),
            pltpu.VMEM((2, 2, 128), F32),
            pltpu.VMEM((2, 512, 128), BF),
            pltpu.VMEM((6, 256, 256), BF),
            pltpu.VMEM((2, 2, 512, 128), BF),
            pltpu.VMEM((2, 512, 128), BF),
            pltpu.VMEM((2, 128, 1024), BF),
            pltpu.VMEM((2, 128, 8, 128), BF),
            pltpu.VMEM((128, 8, 128), BF),
            pltpu.VMEM((256, 8, 128), BF),
            pltpu.VMEM((256, 512), BF),
            pltpu.VMEM((512, 512), BF),
            pltpu.VMEM((2, 256, 256), BF),
            pltpu.VMEM((128, 8, 128), BF),
            pltpu.VMEM((128, 8, 128), BF),
            pltpu.VMEM((128, 16, 128), BF),
            pltpu.VMEM((128, 16, 128), BF),
            pltpu.VMEM((2, 256, 512), BF),
            pltpu.VMEM((256, 8, 128), BF),
            pltpu.VMEM((2, 128, 8, 128), BF),
            pltpu.VMEM((128, 1024), F32),
        ]
        + [pltpu.SemaphoreType.DMA] * 10
        + [
            pltpu.SemaphoreType.DMA((6,)),
        ],
        compiler_params=pltpu.CompilerParams(
            collective_id=0, has_side_effects=True, vmem_limit_bytes=40 * 1024 * 1024
        ),
        name="triangles",
    )(pair_map, pair_mask, edge_weights, gate_weights, out_weights, norm_gains)


def solution(mesh):
    return jax.shard_map(
        per_device,
        mesh=mesh,
        in_specs=(P(("dap", "grp"), None, None), P(("dap", "grp"), None), P(), P(), P(), P()),
        out_specs=P(("dap", "grp"), None, None),
        check_vma=False,
    )
```

time: 73.6 us -> 74.8 us (1.016)
  Pallas kernels: 67.6 us -> 68.9 us
    pallas_call x1, Pallas kernels: 67.6 us -> 68.9 us  [per_device(): pl.pallas_call(kernel, out_shape=jax.ShapeDtypeStruct((2, 512, 128), BF),...]
where the time goes in v6:
time: 74.8 us; the launch traced here: 74.6 us
  Pallas kernels  68.9 us (92%)
  local copies, waits for them, and re-layouts  5.65 us (8%)
    pallas_call x1, Pallas kernels, per_device(): pl.pallas_call(kernel, out_shape=jax.ShapeDtypeStruct((2, 512, 128), BF),...  68.9 us
    unnamed x13, local copies, waits for them, and re-layouts  5.65 us

profile of v6, /device:TPU:1, one launch (start us, length us, event | category | flops | bytes accessed | tf_op | source)
XLA Modules:
  0.0 74.6 jit_solution(5050985934016517440)
XLA Ops:
  0.0 0.0 copy-start
  0.0 0.9 %copy-done = bf16[2,512,128]{2,1,0:T(8,128)(2,1)S(1)} copy-done((bf16[2,512,128]{2,1,0:T(8,128)(2,1)S(1)}, bf16[2,512,128]{2,1,0:T(8,128)(2,1)}, u32[]{:S(2)}) %copy-start) | copy-done | bytes 262168
  1.0 0.0 copy-start.1
  1.0 0.9 %copy-done.1 = bf16[2,128,512]{2,1,0:T(8,128)(2,1)S(1)} copy-done((bf16[2,128,512]{2,1,0:T(8,128)(2,1)S(1)}, bf16[2,128,512]{2,1,0:T(8,128)(2,1)}, u32[]{:S(2)}) %copy-start.1) | copy-done | bytes 262168
  1.9 0.0 copy-start.2
  1.9 0.8 %copy-done.2 = bf16[2,128,128]{2,1,0:T(8,128)(2,1)S(1)} copy-done((bf16[2,128,128]{2,1,0:T(8,128)(2,1)S(1)}, bf16[2,128,128]{2,1,0:T(8,128)(2,1)}, u32[]{:S(2)}) %copy-start.2) | copy-done | bytes 65560
  2.7 0.0 copy-start.3
  2.7 0.8 %copy-done.3 = bf16[2,128,128]{2,1,0:T(8,128)(2,1)S(1)} copy-done((bf16[2,128,128]{2,1,0:T(8,128)(2,1)S(1)}, bf16[2,128,128]{2,1,0:T(8,128)(2,1)}, u32[]{:S(2)}) %copy-start.3) | copy-done | bytes 65560
  3.6 0.0 copy-start.4
  3.6 0.7 copy-done.4
  4.3 0.0 copy-start.5
  4.3 0.7 copy-done.5
  5.0 68.9 %triangles.1 = bf16[2,512,128]{2,1,0:T(8,128)(2,1)S(1)} custom-call(bf16[2,512,128]{2,1,0:T(8,128)(2,1)S(1)} %copy-done, s32[2,512]{1,0:T(2,128)S(1)} %copy-done.4, bf16[2,128,512]{2,1,0:T(8,128)(2,1)S(1)} %copy-done.1, bf16[2,128,128]{2,1,0:T(8,128)(2,1)S(1)} %copy-done.2, bf16[2,128,128]{2,1,0:T(8,128)(2,1)S(1)} %copy-done.3, f32[2,2,128]{2,1,0:T(2,128)S(1)} %copy-done.5), custom_call_target="tpu_custom_call" | custom-call | tf_op jit(solution)/shard_map/triangles/pallas_call | solution.py:258
  73.9 0.7 copy.8
Async XLA Ops:
  0.0 0.9 %copy-start = (bf16[2,512,128]{2,1,0:T(8,128)(2,1)S(1)}, bf16[2,512,128]{2,1,0:T(8,128)(2,1)}, u32[]{:S(2)}) copy-start(bf16[2,512,128]{2,1,0:T(8,128)(2,1)} %z_hbm.1) | copy-start | bytes 786436
  1.0 0.9 %copy-start.1 = (bf16[2,128,512]{2,1,0:T(8,128)(2,1)S(1)}, bf16[2,128,512]{2,1,0:T(8,128)(2,1)}, u32[]{:S(2)}) copy-start(bf16[2,128,512]{2,1,0:T(8,128)(2,1)} %we_hbm.1) | copy-start | bytes 786436
  1.9 0.8 %copy-start.2 = (bf16[2,128,128]{2,1,0:T(8,128)(2,1)S(1)}, bf16[2,128,128]{2,1,0:T(8,128)(2,1)}, u32[]{:S(2)}) copy-start(bf16[2,128,128]{2,1,0:T(8,128)(2,1)} %wg_hbm.1) | copy-start | bytes 196612
  2.7 0.8 %copy-start.3 = (bf16[2,128,128]{2,1,0:T(8,128)(2,1)S(1)}, bf16[2,128,128]{2,1,0:T(8,128)(2,1)}, u32[]{:S(2)}) copy-start(bf16[2,128,128]{2,1,0:T(8,128)(2,1)} %wo_hbm.1) | copy-start | bytes 196612
  3.6 0.7 copy-start.4
  4.3 0.7 copy-start.5

commit v7 on v5

--- a/solution.py
+++ b/solution.py
@@ -44,9 +44,9 @@
     return (number >> 2, number & 3)
 
 
-def kernel(z_hbm, mask_hbm, we_hbm, wg_hbm, wo_hbm, gains_hbm, out_ref,
-           z_ref, mask_ref, we_ref, wg_ref, wo_ref, gains_ref, wt, perms, normed, cur, edges, send1, recv1, left, right, prod, send2, recv2,
-           send3, recv3, pairs, send4, recv4, chan, s1, r1, s2, r2, s3, r3, s4, r4, sx, rx, load):
+def kernel(z_hbm, mask_hbm, we_hbm, wg_hbm, wo_hbm, gains_hbm, out_hbm,
+           z_ref, mask_ref, we_ref, wg_ref, wo_ref, gains_ref, wt, perms, normed, cur, edges, send1, recv1, left, right, send2, recv2,
+           send3, recv3, pairs, send4, recv4, chan, result, s1, r1, s2, r2, s3, r3, s4, r4, sx, rx, load, store):
     dap = lax.axis_index("dap")
     number = dap * 4 + lax.axis_index("grp")
     core = (number >> 2) & 1
@@ -67,14 +67,14 @@
 
     barrier = pltpu.get_barrier_semaphore()
 
-    def partners(visit):
+    def partners(visit, masks=XY_MASKS):
         word = jnp.where(zlo == core, packed(Z_EVEN), packed(Z_ODD))
         chip = number - core * 4
 
         def one(k, carry):
             z = nibble(word, k & 3)
             base = chip ^ (((z >> 3) << 7) | (z & 3) | ((k >> 2) << 2))
-            for mx, my in XY_MASKS:
+            for mx, my in masks:
                 visit(base ^ (my << 5 | mx << 3))
             return carry
 
@@ -123,13 +123,20 @@
             stack = jnp.concatenate([edges[lr, rows, j * 128 : j * 128 + 128] for j in range(8)], axis=0)
             send1[lr, rows] = dot(perms[0], stack, 1, 0).reshape(32, 8, 128).astype(BF)
 
-    def pack_both():
-        for b in range(8):
+    def edges_of(base):
+        for p in range(4):
+            row, lanes = p // 2, slice(p % 2 * 256, p % 2 * 256 + 256)
+            mask = mask_ref[row : row + 1, lanes].astype(F32)
+            for lr in range(2):
+                gate = dot(wt[1, pl.ds(base + lr * 256, 64), :], normed[1, row, lanes, :], 1, 1)
+                value = dot(wt[1, pl.ds(base + lr * 256 + 128, 64), :], normed[1, row, lanes, :], 1, 1)
+                edges[lr, 0:64, p * 256 : p * 256 + 256] = (jax.nn.sigmoid(gate) * value * mask).astype(BF)
+        for b in range(4):
             rows = slice(b * 16, b * 16 + 16)
             stack = jnp.concatenate(
                 [edges[lr, rows, j * 128 : j * 128 + 128] for lr in range(2) for j in range(8)], axis=0
             )
-            send3[rows] = dot(perms[4], stack, 1, 0).astype(BF).reshape(16, 16, 128)
+            send3[pl.ds(base + b * 16, 16)] = dot(perms[4], stack, 1, 0).astype(BF).reshape(16, 16, 128)
 
     def scatter_edges(lr):
         base = (number - core * 4) | (zlo << 2)
@@ -157,7 +164,7 @@
 
         lax.fori_loop(0, 8, one, 0)
 
-    def scatter_products():
+    def scatter_products(masks):
         def send(other):
             at = other & 127
 
@@ -172,18 +179,18 @@
             def _():
                 pltpu.make_async_copy(send2.at[at], recv2.at[channel], r2).start()
 
-        partners(send)
+        partners(send, masks)
 
     mine = ((number >> 2) << 1) | (number & 1)
 
-    def scatter_pairs():
+    def scatter_pairs(odd):
         z = ((number & 3) << 1) | zlo
         plane = number & (15 << 3)
 
         def one(k, carry):
             worker_core = k & 1
             step = k >> 1
-            dz = jnp.where(step == 0, 2 + 4 * worker_core, jnp.where(step == 1, 1, jnp.where(step == 2, 7, 0)))
+            dz = jnp.where(step == 0, 1, 7) if odd else jnp.where(step == 0, 2 + 4 * worker_core, 0)
             wz = (z + dz) & 7
             base = ((wz & 1) << 7) | plane | (worker_core << 2) | (wz >> 1)
             for mx, my in XY_MASKS:
@@ -204,14 +211,13 @@
 
             return carry
 
-        lax.fori_loop(0, 8, one, 0)
-
-    def scatter_parts():
+        lax.fori_loop(0, 4, one, 0)
+
+    def scatter_parts(masks):
         part = (number >> 1) & 1
 
         def one(k, carry):
-            zk = k >> 1
-            z = jnp.where(zk == 7, 0, nibble(packed(Z_MASKS), zk))
+            z = nibble(packed(masks), k >> 1)
             base = number ^ (((z >> 3) << 7) | (z & 3) | ((k & 1) << 2))
             for mx, my in XY_MASKS:
                 other = base ^ (my << 5 | mx << 3)
@@ -230,7 +236,7 @@
 
             return carry
 
-        lax.fori_loop(0, 16, one, 0)
+        lax.fori_loop(0, 8, one, 0)
 
     def wait_all(buf, sem):
         pltpu.make_async_copy(buf, buf, sem).wait()
@@ -258,16 +264,17 @@
         for b in range(4):
             for k, block in enumerate(gathered(0, b)):
                 left[b * 64 : b * 64 + 64, k * 128 : k * 128 + 128] = block
-        for step in range(2):
-            if step == 1:
-                relay.wait_recv()
-            half = core if step == 0 else 1 - core
-            prod[half] = dot(left[...], right[half], 1, 1).astype(BF)
-        for b in range(4):
-            rows = slice(b * 64, b * 64 + 64)
-            send2[b * 32 : b * 32 + 32] = messages(
-                [prod[j // 2, rows, (j % 2) * 128 : (j % 2) * 128 + 128] for j in range(4)]
-            )
+        relay.wait_recv()
+        top = (number >> 6) & 1
+        for flip in (1, 0):
+            first = pl.multiple_of((top ^ flip) * 128, 128)
+            rows = left[pl.ds(first, 128), :]
+            halves = [dot(rows, right[j], 1, 1).astype(BF) for j in range(2)]
+            for b in range(2):
+                send2[pl.ds((top ^ flip) * 64 + b * 32, 32)] = messages(
+                    [halves[j // 2][b * 64 : b * 64 + 64, (j % 2) * 128 : (j % 2) * 128 + 128] for j in range(4)]
+                )
+            scatter_products([m for m in XY_MASKS if m[1] >> 1 == flip])
         return relay
 
     def multiply_incoming():
@@ -280,12 +287,15 @@
                     pairs[lr, b * 32 : b * 32 + 32, k * 128 : k * 128 + 128] = blocks[
                         lr * 128 + k * 32 : lr * 128 + k * 32 + 32
                     ]
-        for i in range(2):
-            part = dot(pairs[0, :, i * 256 : i * 256 + 256], pairs[1], 0, 0).astype(BF)
+        for masks, flip in ((Z_EVEN, 0), (Z_ODD, 1)):
+            half = zlo ^ flip
+            lhs = pairs[0, :, pl.ds(pl.multiple_of(half * 256, 256), 256)]
+            part = dot(lhs, pairs[1], 0, 0).astype(BF)
             for b in range(4):
-                send4[i * 128 + b * 32 : i * 128 + b * 32 + 32] = messages(
+                send4[pl.ds(half * 128 + b * 32, 32)] = messages(
                     [part[b * 64 : b * 64 + 64, j * 128 : j * 128 + 128] for j in range(4)]
                 )
+            scatter_parts(masks)
 
     def by_channel(buf, b):
         block = buf[b * 32 : b * 32 + 32].astype(F32).reshape(256, 128).astype(BF)
@@ -313,9 +323,13 @@
             scaled = (centred * lax.rsqrt(variance + 1e-05) * gain).astype(BF)
             projected = dot(scaled, wo_ref[u], 0, 0)
             gating = jax.nn.sigmoid(dot(normed[u, row, lanes, :], wg_ref[u], 1, 0))
-            result = source[row, lanes, :].astype(F32) + gating * projected
-            target[row, lanes, :] = result.astype(BF)
-
+            updated = source[row, lanes, :].astype(F32) + gating * projected
+            target[row, lanes, :] = updated.astype(BF)
+            if u == 1:
+                stores.append(pltpu.make_async_copy(target.at[row, lanes], out_hbm.at[row, lanes], store.at[p]))
+                stores[-1].start()
+
+    stores = []
     normalize_rows(0, z_ref)
     for lr in (1, 0):
         edge_map(0, lr)
@@ -324,18 +338,18 @@
     scatter_edges(1)
     scatter_edges(0)
     relay = multiply_outgoing()
-    scatter_products()
     finish(0, z_ref, cur)
 
     normalize_rows(1, cur)
-    edge_map(1, 0)
-    edge_map(1, 1)
-    pack_both()
-    scatter_pairs()
+    edges_of(pl.multiple_of(zlo * 64, 64))
+    scatter_pairs(False)
+    edges_of(pl.multiple_of((1 - zlo) * 64, 64))
+    scatter_pairs(True)
     multiply_incoming()
-    scatter_parts()
-    finish(1, cur, out_ref)
-
+    finish(1, cur, result)
+
+    for copy in stores:
+        copy.wait()
     relay.wait_send()
     wait_all(send3.at[pl.ds(0, 127)], s3)
     wait_all(send4.at[pl.ds(0, 255)], s4)
@@ -354,12 +368,11 @@
 
 
 def per_device(pair_map, pair_mask, edge_weights, gate_weights, out_weights, norm_gains):
-    vmem = pl.BlockSpec(memory_space=pltpu.VMEM)
     return pl.pallas_call(
         kernel,
         out_shape=jax.ShapeDtypeStruct((2, 512, 128), BF),
         in_specs=[pl.BlockSpec(memory_space=pl.ANY)] * 6,
-        out_specs=vmem,
+        out_specs=pl.BlockSpec(memory_space=pl.ANY),
         scratch_shapes=[
             pltpu.VMEM((2, 512, 128), BF),
             pltpu.VMEM((2, 512), jnp.int32),
@@ -376,7 +389,6 @@
             pltpu.VMEM((2, 128, 8, 128), BF),
             pltpu.VMEM((256, 512), BF),
             pltpu.VMEM((2, 256, 512), BF),
-            pltpu.VMEM((2, 256, 256), BF),
             pltpu.VMEM((128, 8, 128), BF),
             pltpu.VMEM((128, 8, 128), BF),
             pltpu.VMEM((128, 16, 128), BF),
@@ -385,12 +397,14 @@
             pltpu.VMEM((256, 8, 128), BF),
             pltpu.VMEM((2, 128, 8, 128), BF),
             pltpu.VMEM((128, 1024), F32),
+            pltpu.VMEM((2, 512, 128), BF),
             pltpu.SemaphoreType.DMA((2,)),
             pltpu.SemaphoreType.DMA((2,)),
         ]
         + [pltpu.SemaphoreType.DMA] * 8
         + [
             pltpu.SemaphoreType.DMA((6,)),
+            pltpu.SemaphoreType.DMA((4,)),
         ],
         compiler_params=pltpu.CompilerParams(
             collective_id=0, has_side_effects=True, vmem_limit_bytes=40 * 1024 * 1024

time: 73.6 us -> 75 us (1.019)
  Pallas kernels: 67.6 us -> 69 us
    pallas_call x1, Pallas kernels: 67.6 us -> 69 us  [per_device(): pl.pallas_call(kernel, out_shape=jax.ShapeDtypeStruct((2, 512, 128), BF),...]
where the time goes in v7:
time: 75 us; the launch traced here: 74.7 us
  Pallas kernels  69 us (92%)
  local copies, waits for them, and re-layouts  5.65 us (8%)
    pallas_call x1, Pallas kernels, per_device(): pl.pallas_call(kernel, out_shape=jax.ShapeDtypeStruct((2, 512, 128), BF),...  69 us
    unnamed x13, local copies, waits for them, and re-layouts  5.65 us

profile of v7, /device:TPU:1, one launch (start us, length us, event | category | flops | bytes accessed | tf_op | source)
XLA Modules:
  0.0 74.7 jit_solution(12761775596732884682)
XLA Ops:
  0.0 0.0 copy-start
  0.0 0.9 %copy-done = bf16[2,512,128]{2,1,0:T(8,128)(2,1)S(1)} copy-done((bf16[2,512,128]{2,1,0:T(8,128)(2,1)S(1)}, bf16[2,512,128]{2,1,0:T(8,128)(2,1)}, u32[]{:S(2)}) %copy-start) | copy-done | bytes 262168
  1.0 0.0 copy-start.1
  1.0 0.9 %copy-done.1 = bf16[2,128,512]{2,1,0:T(8,128)(2,1)S(1)} copy-done((bf16[2,128,512]{2,1,0:T(8,128)(2,1)S(1)}, bf16[2,128,512]{2,1,0:T(8,128)(2,1)}, u32[]{:S(2)}) %copy-start.1) | copy-done | bytes 262168
  1.9 0.0 copy-start.2
  1.9 0.8 %copy-done.2 = bf16[2,128,128]{2,1,0:T(8,128)(2,1)S(1)} copy-done((bf16[2,128,128]{2,1,0:T(8,128)(2,1)S(1)}, bf16[2,128,128]{2,1,0:T(8,128)(2,1)}, u32[]{:S(2)}) %copy-start.2) | copy-done | bytes 65560
  2.7 0.0 copy-start.3
  2.7 0.8 %copy-done.3 = bf16[2,128,128]{2,1,0:T(8,128)(2,1)S(1)} copy-done((bf16[2,128,128]{2,1,0:T(8,128)(2,1)S(1)}, bf16[2,128,128]{2,1,0:T(8,128)(2,1)}, u32[]{:S(2)}) %copy-start.3) | copy-done | bytes 65560
  3.6 0.0 copy-start.4
  3.6 0.7 copy-done.4
  4.3 0.0 copy-start.5
  4.3 0.7 copy-done.5
  5.0 69.0 %triangles.1 = bf16[2,512,128]{2,1,0:T(8,128)(2,1)S(1)} custom-call(bf16[2,512,128]{2,1,0:T(8,128)(2,1)S(1)} %copy-done, s32[2,512]{1,0:T(2,128)S(1)} %copy-done.4, bf16[2,128,512]{2,1,0:T(8,128)(2,1)S(1)} %copy-done.1, bf16[2,128,128]{2,1,0:T(8,128)(2,1)S(1)} %copy-done.2, bf16[2,128,128]{2,1,0:T(8,128)(2,1)S(1)} %copy-done.3, f32[2,2,128]{2,1,0:T(2,128)S(1)} %copy-done.5), custom_call_target="tpu_custom_call" | custom-call | tf_op jit(solution)/shard_map/triangles/pallas_call | solution.py:371
  74.0 0.7 copy.8
Async XLA Ops:
  0.0 0.9 %copy-start = (bf16[2,512,128]{2,1,0:T(8,128)(2,1)S(1)}, bf16[2,512,128]{2,1,0:T(8,128)(2,1)}, u32[]{:S(2)}) copy-start(bf16[2,512,128]{2,1,0:T(8,128)(2,1)} %z_hbm.1) | copy-start | bytes 786436
  1.0 0.9 %copy-start.1 = (bf16[2,128,512]{2,1,0:T(8,128)(2,1)S(1)}, bf16[2,128,512]{2,1,0:T(8,128)(2,1)}, u32[]{:S(2)}) copy-start(bf16[2,128,512]{2,1,0:T(8,128)(2,1)} %we_hbm.1) | copy-start | bytes 786436
  1.9 0.8 %copy-start.2 = (bf16[2,128,128]{2,1,0:T(8,128)(2,1)S(1)}, bf16[2,128,128]{2,1,0:T(8,128)(2,1)}, u32[]{:S(2)}) copy-start(bf16[2,128,128]{2,1,0:T(8,128)(2,1)} %wg_hbm.1) | copy-start | bytes 196612
  2.7 0.8 %copy-start.3 = (bf16[2,128,128]{2,1,0:T(8,128)(2,1)S(1)}, bf16[2,128,128]{2,1,0:T(8,128)(2,1)}, u32[]{:S(2)}) copy-start(bf16[2,128,128]{2,1,0:T(8,128)(2,1)} %wo_hbm.1) | copy-start | bytes 196612
  3.6 0.7 copy-start.4
  4.3 0.7 copy-start.5

commit v8 on v7

--- a/solution.py
+++ b/solution.py
@@ -44,9 +44,9 @@
     return (number >> 2, number & 3)
 
 
-def kernel(z_hbm, mask_hbm, we_hbm, wg_hbm, wo_hbm, gains_hbm, out_hbm,
+def kernel(z_hbm, mask_hbm, we_hbm, wg_hbm, wo_hbm, gains_hbm, out_ref,
            z_ref, mask_ref, we_ref, wg_ref, wo_ref, gains_ref, wt, perms, normed, cur, edges, send1, recv1, left, right, send2, recv2,
-           send3, recv3, pairs, send4, recv4, chan, result, s1, r1, s2, r2, s3, r3, s4, r4, sx, rx, load, store):
+           send3, recv3, pairs, send4, recv4, chan, s1, r1, s2, r2, s3, r3, s4, r4, sx, rx, load):
     dap = lax.axis_index("dap")
     number = dap * 4 + lax.axis_index("grp")
     core = (number >> 2) & 1
@@ -124,12 +124,13 @@
             send1[lr, rows] = dot(perms[0], stack, 1, 0).reshape(32, 8, 128).astype(BF)
 
     def edges_of(base):
+        weights = jnp.concatenate([wt[1, pl.ds(base + c * 128, 64), :] for c in range(4)], axis=0)
         for p in range(4):
             row, lanes = p // 2, slice(p % 2 * 256, p % 2 * 256 + 256)
             mask = mask_ref[row : row + 1, lanes].astype(F32)
+            proj = dot(weights, normed[1, row, lanes, :], 1, 1)
             for lr in range(2):
-                gate = dot(wt[1, pl.ds(base + lr * 256, 64), :], normed[1, row, lanes, :], 1, 1)
-                value = dot(wt[1, pl.ds(base + lr * 256 + 128, 64), :], normed[1, row, lanes, :], 1, 1)
+                gate, value = proj[lr * 128 : lr * 128 + 64], proj[lr * 128 + 64 : lr * 128 + 128]
                 edges[lr, 0:64, p * 256 : p * 256 + 256] = (jax.nn.sigmoid(gate) * value * mask).astype(BF)
         for b in range(4):
             rows = slice(b * 16, b * 16 + 16)
@@ -217,9 +218,10 @@
         part = (number >> 1) & 1
 
         def one(k, carry):
-            z = nibble(packed(masks), k >> 1)
+            zk = k >> 1
+            z = jnp.where(zk == 7, 0, nibble(packed(Z_MASKS), zk))
             base = number ^ (((z >> 3) << 7) | (z & 3) | ((k & 1) << 2))
-            for mx, my in XY_MASKS:
+            for mx, my in masks:
                 other = base ^ (my << 5 | mx << 3)
                 copy = pltpu.make_async_remote_copy(
                     src_ref=send4.at[other], dst_ref=recv4.at[part, mine], send_sem=s4, recv_sem=r4,
@@ -236,7 +238,7 @@
 
             return carry
 
-        lax.fori_loop(0, 8, one, 0)
+        lax.fori_loop(0, 16, one, 0)
 
     def wait_all(buf, sem):
         pltpu.make_async_copy(buf, buf, sem).wait()
@@ -287,15 +289,18 @@
                     pairs[lr, b * 32 : b * 32 + 32, k * 128 : k * 128 + 128] = blocks[
                         lr * 128 + k * 32 : lr * 128 + k * 32 + 32
                     ]
-        for masks, flip in ((Z_EVEN, 0), (Z_ODD, 1)):
-            half = zlo ^ flip
-            lhs = pairs[0, :, pl.ds(pl.multiple_of(half * 256, 256), 256)]
+        top = (number >> 6) & 1
+        for flip in (1, 0):
+            y1 = top ^ flip
+            lhs = jnp.concatenate(
+                [pairs[0, :, pl.ds(pl.multiple_of(zl * 256 + y1 * 128, 128), 128)] for zl in range(2)], axis=1
+            )
             part = dot(lhs, pairs[1], 0, 0).astype(BF)
             for b in range(4):
-                send4[pl.ds(half * 128 + b * 32, 32)] = messages(
+                send4[pl.ds((b // 2) * 128 + y1 * 64 + (b % 2) * 32, 32)] = messages(
                     [part[b * 64 : b * 64 + 64, j * 128 : j * 128 + 128] for j in range(4)]
                 )
-            scatter_parts(masks)
+            scatter_parts([m for m in XY_MASKS if m[1] >> 1 == flip])
 
     def by_channel(buf, b):
         block = buf[b * 32 : b * 32 + 32].astype(F32).reshape(256, 128).astype(BF)
@@ -325,11 +330,7 @@
             gating = jax.nn.sigmoid(dot(normed[u, row, lanes, :], wg_ref[u], 1, 0))
             updated = source[row, lanes, :].astype(F32) + gating * projected
             target[row, lanes, :] = updated.astype(BF)
-            if u == 1:
-                stores.append(pltpu.make_async_copy(target.at[row, lanes], out_hbm.at[row, lanes], store.at[p]))
-                stores[-1].start()
-
-    stores = []
+
     normalize_rows(0, z_ref)
     for lr in (1, 0):
         edge_map(0, lr)
@@ -346,10 +347,8 @@
     edges_of(pl.multiple_of((1 - zlo) * 64, 64))
     scatter_pairs(True)
     multiply_incoming()
-    finish(1, cur, result)
-
-    for copy in stores:
-        copy.wait()
+    finish(1, cur, out_ref)
+
     relay.wait_send()
     wait_all(send3.at[pl.ds(0, 127)], s3)
     wait_all(send4.at[pl.ds(0, 255)], s4)
@@ -372,7 +371,7 @@
         kernel,
         out_shape=jax.ShapeDtypeStruct((2, 512, 128), BF),
         in_specs=[pl.BlockSpec(memory_space=pl.ANY)] * 6,
-        out_specs=pl.BlockSpec(memory_space=pl.ANY),
+        out_specs=pl.BlockSpec(memory_space=pltpu.VMEM),
         scratch_shapes=[
             pltpu.VMEM((2, 512, 128), BF),
             pltpu.VMEM((2, 512), jnp.int32),
@@ -397,14 +396,12 @@
             pltpu.VMEM((256, 8, 128), BF),
             pltpu.VMEM((2, 128, 8, 128), BF),
             pltpu.VMEM((128, 1024), F32),
-            pltpu.VMEM((2, 512, 128), BF),
             pltpu.SemaphoreType.DMA((2,)),
             pltpu.SemaphoreType.DMA((2,)),
         ]
         + [pltpu.SemaphoreType.DMA] * 8
         + [
             pltpu.SemaphoreType.DMA((6,)),
-            pltpu.SemaphoreType.DMA((4,)),
         ],
         compiler_params=pltpu.CompilerParams(
             collective_id=0, has_side_effects=True, vmem_limit_bytes=40 * 1024 * 1024

time: 75 us -> 72.3 us (0.964)
  Pallas kernels: 69 us -> 66.3 us
    pallas_call x1, Pallas kernels: 69 us -> 66.3 us  [per_device(): pl.pallas_call(kernel, out_shape=jax.ShapeDtypeStruct((2, 512, 128), BF),...]
where the time goes in v8:
time: 72.3 us; the launch traced here: 72 us
  Pallas kernels  66.3 us (92%)
  local copies, waits for them, and re-layouts  5.65 us (8%)
    pallas_call x1, Pallas kernels, per_device(): pl.pallas_call(kernel, out_shape=jax.ShapeDtypeStruct((2, 512, 128), BF),...  66.3 us
    unnamed x13, local copies, waits for them, and re-layouts  5.65 us

profile of v8, /device:TPU:1, one launch (start us, length us, event | category | flops | bytes accessed | tf_op | source)
XLA Modules:
  0.0 72.0 jit_solution(12218718256570814681)
XLA Ops:
  0.0 0.0 copy-start
  0.0 0.9 %copy-done = bf16[2,512,128]{2,1,0:T(8,128)(2,1)S(1)} copy-done((bf16[2,512,128]{2,1,0:T(8,128)(2,1)S(1)}, bf16[2,512,128]{2,1,0:T(8,128)(2,1)}, u32[]{:S(2)}) %copy-start) | copy-done | bytes 262168
  1.0 0.0 copy-start.1
  1.0 0.9 %copy-done.1 = bf16[2,128,512]{2,1,0:T(8,128)(2,1)S(1)} copy-done((bf16[2,128,512]{2,1,0:T(8,128)(2,1)S(1)}, bf16[2,128,512]{2,1,0:T(8,128)(2,1)}, u32[]{:S(2)}) %copy-start.1) | copy-done | bytes 262168
  1.9 0.0 copy-start.2
  1.9 0.8 %copy-done.2 = bf16[2,128,128]{2,1,0:T(8,128)(2,1)S(1)} copy-done((bf16[2,128,128]{2,1,0:T(8,128)(2,1)S(1)}, bf16[2,128,128]{2,1,0:T(8,128)(2,1)}, u32[]{:S(2)}) %copy-start.2) | copy-done | bytes 65560
  2.7 0.0 copy-start.3
  2.7 0.8 %copy-done.3 = bf16[2,128,128]{2,1,0:T(8,128)(2,1)S(1)} copy-done((bf16[2,128,128]{2,1,0:T(8,128)(2,1)S(1)}, bf16[2,128,128]{2,1,0:T(8,128)(2,1)}, u32[]{:S(2)}) %copy-start.3) | copy-done | bytes 65560
  3.6 0.0 copy-start.4
  3.6 0.7 copy-done.4
  4.3 0.0 copy-start.5
  4.3 0.7 copy-done.5
  5.0 66.3 %triangles.1 = bf16[2,512,128]{2,1,0:T(8,128)(2,1)S(1)} custom-call(bf16[2,512,128]{2,1,0:T(8,128)(2,1)S(1)} %copy-done, s32[2,512]{1,0:T(2,128)S(1)} %copy-done.4, bf16[2,128,512]{2,1,0:T(8,128)(2,1)S(1)} %copy-done.1, bf16[2,128,128]{2,1,0:T(8,128)(2,1)S(1)} %copy-done.2, bf16[2,128,128]{2,1,0:T(8,128)(2,1)S(1)} %copy-done.3, f32[2,2,128]{2,1,0:T(2,128)S(1)} %copy-done.5), custom_call_target="tpu_custom_call" | custom-call | tf_op jit(solution)/shard_map/triangles/pallas_call | solution.py:370
  71.3 0.7 copy.8
Async XLA Ops:
  0.0 0.9 %copy-start = (bf16[2,512,128]{2,1,0:T(8,128)(2,1)S(1)}, bf16[2,512,128]{2,1,0:T(8,128)(2,1)}, u32[]{:S(2)}) copy-start(bf16[2,512,128]{2,1,0:T(8,128)(2,1)} %z_hbm.1) | copy-start | bytes 786436
  1.0 0.9 %copy-start.1 = (bf16[2,128,512]{2,1,0:T(8,128)(2,1)S(1)}, bf16[2,128,512]{2,1,0:T(8,128)(2,1)}, u32[]{:S(2)}) copy-start(bf16[2,128,512]{2,1,0:T(8,128)(2,1)} %we_hbm.1) | copy-start | bytes 786436
  1.9 0.8 %copy-start.2 = (bf16[2,128,128]{2,1,0:T(8,128)(2,1)S(1)}, bf16[2,128,128]{2,1,0:T(8,128)(2,1)}, u32[]{:S(2)}) copy-start(bf16[2,128,128]{2,1,0:T(8,128)(2,1)} %wg_hbm.1) | copy-start | bytes 196612
  2.7 0.8 %copy-start.3 = (bf16[2,128,128]{2,1,0:T(8,128)(2,1)S(1)}, bf16[2,128,128]{2,1,0:T(8,128)(2,1)}, u32[]{:S(2)}) copy-start(bf16[2,128,128]{2,1,0:T(8,128)(2,1)} %wo_hbm.1) | copy-start | bytes 196612
  3.6 0.7 copy-start.4
  4.3 0.7 copy-start.5

commit v9 on v8

--- a/solution.py
+++ b/solution.py
@@ -75,15 +75,19 @@
             z = nibble(word, k & 3)
             base = chip ^ (((z >> 3) << 7) | (z & 3) | ((k >> 2) << 2))
             for mx, my in masks:
-                visit(base ^ (my << 5 | mx << 3))
+                visit(base ^ (my << 5 | mx << 3), mx == 0 and my == 0)
             return carry
 
         lax.fori_loop(0, 8, one, 0)
 
-    def greet(other):
-        @pl.when((other | 4) != (number | 4))
-        def _():
+    def greet(other, maybe_here):
+        def signal():
             pl.semaphore_signal(barrier, inc=1, device_id=mesh_id(other), device_id_type=MESH)
+
+        if maybe_here:
+            pl.when((other | 4) != (number | 4))(signal)
+        else:
+            signal()
 
     pl.semaphore_signal(barrier, inc=1, device_id=sibling, device_id_type=MESH)
     partners(greet)
@@ -166,15 +170,16 @@
         lax.fori_loop(0, 8, one, 0)
 
     def scatter_products(masks):
-        def send(other):
+        def send(other, maybe_self):
             at = other & 127
-
-            @pl.when(other != number)
-            def _():
-                pltpu.make_async_remote_copy(
-                    src_ref=send2.at[at], dst_ref=recv2.at[channel], send_sem=s2, recv_sem=r2,
-                    device_id=mesh_id(other), device_id_type=MESH,
-                ).start()
+            copy = pltpu.make_async_remote_copy(
+                src_ref=send2.at[at], dst_ref=recv2.at[channel], send_sem=s2, recv_sem=r2,
+                device_id=mesh_id(other), device_id_type=MESH,
+            )
+            if not maybe_self:
+                copy.start()
+                return
+            pl.when(other != number)(copy.start)
 
             @pl.when(other == number)
             def _():
@@ -244,7 +249,7 @@
         pltpu.make_async_copy(buf, buf, sem).wait()
 
     def gathered(lr, b):
-        wanted = recv1[lr, b * 32 : b * 32 + 32].astype(F32).reshape(256, 128).astype(BF)
+        wanted = recv1[lr, pl.ds(b * 32, 32)].astype(F32).reshape(256, 128).astype(BF)
         blocks = dot(perms[1], wanted, 1, 0).astype(BF)
         return [blocks[k * 64 : k * 64 + 64] for k in range(4)]
 
@@ -263,14 +268,14 @@
         )
         relay.start()
         wait_all(recv1.at[0], r1.at[0])
-        for b in range(4):
-            for k, block in enumerate(gathered(0, b)):
-                left[b * 64 : b * 64 + 64, k * 128 : k * 128 + 128] = block
-        relay.wait_recv()
         top = (number >> 6) & 1
         for flip in (1, 0):
-            first = pl.multiple_of((top ^ flip) * 128, 128)
-            rows = left[pl.ds(first, 128), :]
+            for b in range(2):
+                for k, block in enumerate(gathered(0, (top ^ flip) * 2 + b)):
+                    left[flip, b * 64 : b * 64 + 64, k * 128 : k * 128 + 128] = block
+            rows = left[flip]
+            if flip:
+                relay.wait_recv()
             halves = [dot(rows, right[j], 1, 1).astype(BF) for j in range(2)]
             for b in range(2):
                 send2[pl.ds((top ^ flip) * 64 + b * 32, 32)] = messages(
@@ -386,7 +391,7 @@
             pltpu.VMEM((2, 128, 1024), BF),
             pltpu.VMEM((2, 128, 8, 128), BF),
             pltpu.VMEM((2, 128, 8, 128), BF),
-            pltpu.VMEM((256, 512), BF),
+            pltpu.VMEM((2, 128, 512), BF),
             pltpu.VMEM((2, 256, 512), BF),
             pltpu.VMEM((128, 8, 128), BF),
             pltpu.VMEM((128, 8, 128), BF),

time: 72.3 us -> 72.3 us (level)
  no operation moved by 1% of the time
where the time goes in v9:
time: 72.3 us; the launch traced here: 72 us
  Pallas kernels  66.3 us (92%)
  local copies, waits for them, and re-layouts  5.65 us (8%)
    pallas_call x1, Pallas kernels, per_device(): pl.pallas_call(kernel, out_shape=jax.ShapeDtypeStruct((2, 512, 128), BF),...  66.3 us
    unnamed x13, local copies, waits for them, and re-layouts  5.65 us

profile of v9, /device:TPU:1, one launch (start us, length us, event | category | flops | bytes accessed | tf_op | source)
XLA Modules:
  0.0 72.0 jit_solution(9428945697224611153)
XLA Ops:
  0.0 0.0 copy-start
  0.0 0.9 %copy-done = bf16[2,512,128]{2,1,0:T(8,128)(2,1)S(1)} copy-done((bf16[2,512,128]{2,1,0:T(8,128)(2,1)S(1)}, bf16[2,512,128]{2,1,0:T(8,128)(2,1)}, u32[]{:S(2)}) %copy-start) | copy-done | bytes 262168
  1.0 0.0 copy-start.1
  1.0 0.9 %copy-done.1 = bf16[2,128,512]{2,1,0:T(8,128)(2,1)S(1)} copy-done((bf16[2,128,512]{2,1,0:T(8,128)(2,1)S(1)}, bf16[2,128,512]{2,1,0:T(8,128)(2,1)}, u32[]{:S(2)}) %copy-start.1) | copy-done | bytes 262168
  1.9 0.0 copy-start.2
  1.9 0.8 %copy-done.2 = bf16[2,128,128]{2,1,0:T(8,128)(2,1)S(1)} copy-done((bf16[2,128,128]{2,1,0:T(8,128)(2,1)S(1)}, bf16[2,128,128]{2,1,0:T(8,128)(2,1)}, u32[]{:S(2)}) %copy-start.2) | copy-done | bytes 65560
  2.7 0.0 copy-start.3
  2.7 0.8 %copy-done.3 = bf16[2,128,128]{2,1,0:T(8,128)(2,1)S(1)} copy-done((bf16[2,128,128]{2,1,0:T(8,128)(2,1)S(1)}, bf16[2,128,128]{2,1,0:T(8,128)(2,1)}, u32[]{:S(2)}) %copy-start.3) | copy-done | bytes 65560
  3.6 0.0 copy-start.4
  3.6 0.7 copy-done.4
  4.3 0.0 copy-start.5
  4.3 0.7 copy-done.5
  5.0 66.3 %triangles.1 = bf16[2,512,128]{2,1,0:T(8,128)(2,1)S(1)} custom-call(bf16[2,512,128]{2,1,0:T(8,128)(2,1)S(1)} %copy-done, s32[2,512]{1,0:T(2,128)S(1)} %copy-done.4, bf16[2,128,512]{2,1,0:T(8,128)(2,1)S(1)} %copy-done.1, bf16[2,128,128]{2,1,0:T(8,128)(2,1)S(1)} %copy-done.2, bf16[2,128,128]{2,1,0:T(8,128)(2,1)S(1)} %copy-done.3, f32[2,2,128]{2,1,0:T(2,128)S(1)} %copy-done.5), custom_call_target="tpu_custom_call" | custom-call | tf_op jit(solution)/shard_map/triangles/pallas_call | solution.py:375
  71.3 0.7 copy.8
Async XLA Ops:
  0.0 0.9 %copy-start = (bf16[2,512,128]{2,1,0:T(8,128)(2,1)S(1)}, bf16[2,512,128]{2,1,0:T(8,128)(2,1)}, u32[]{:S(2)}) copy-start(bf16[2,512,128]{2,1,0:T(8,128)(2,1)} %z_hbm.1) | copy-start | bytes 786436
  1.0 0.9 %copy-start.1 = (bf16[2,128,512]{2,1,0:T(8,128)(2,1)S(1)}, bf16[2,128,512]{2,1,0:T(8,128)(2,1)}, u32[]{:S(2)}) copy-start(bf16[2,128,512]{2,1,0:T(8,128)(2,1)} %we_hbm.1) | copy-start | bytes 786436
  1.9 0.8 %copy-start.2 = (bf16[2,128,128]{2,1,0:T(8,128)(2,1)S(1)}, bf16[2,128,128]{2,1,0:T(8,128)(2,1)}, u32[]{:S(2)}) copy-start(bf16[2,128,128]{2,1,0:T(8,128)(2,1)} %wg_hbm.1) | copy-start | bytes 196612
  2.7 0.8 %copy-start.3 = (bf16[2,128,128]{2,1,0:T(8,128)(2,1)S(1)}, bf16[2,128,128]{2,1,0:T(8,128)(2,1)}, u32[]{:S(2)}) copy-start(bf16[2,128,128]{2,1,0:T(8,128)(2,1)} %wo_hbm.1) | copy-start | bytes 196612
  3.6 0.7 copy-start.4
  4.3 0.7 copy-start.5

commit v10 on v9

--- a/solution.py
+++ b/solution.py
@@ -72,8 +72,8 @@
         chip = number - core * 4
 
         def one(k, carry):
-            z = nibble(word, k & 3)
-            base = chip ^ (((z >> 3) << 7) | (z & 3) | ((k >> 2) << 2))
+            z = nibble(word, k >> 1)
+            base = chip ^ (((z >> 3) << 7) | (z & 3) | ((k & 1) << 2))
             for mx, my in masks:
                 visit(base ^ (my << 5 | mx << 3), mx == 0 and my == 0)
             return carry

time: 72.3 us -> 71.9 us (level)
  no operation moved by 1% of the time
where the time goes in v10:
time: 71.9 us; the launch traced here: 71.7 us
  Pallas kernels  66 us (92%)
  local copies, waits for them, and re-layouts  5.65 us (8%)
    pallas_call x1, Pallas kernels, per_device(): pl.pallas_call(kernel, out_shape=jax.ShapeDtypeStruct((2, 512, 128), BF),...  66 us
    unnamed x13, local copies, waits for them, and re-layouts  5.65 us

profile of v10, /device:TPU:1, one launch (start us, length us, event | category | flops | bytes accessed | tf_op | source)
XLA Modules:
  0.0 71.7 jit_solution(7973508458233322256)
XLA Ops:
  0.0 0.0 copy-start
  0.0 0.9 %copy-done = bf16[2,512,128]{2,1,0:T(8,128)(2,1)S(1)} copy-done((bf16[2,512,128]{2,1,0:T(8,128)(2,1)S(1)}, bf16[2,512,128]{2,1,0:T(8,128)(2,1)}, u32[]{:S(2)}) %copy-start) | copy-done | bytes 262168
  1.0 0.0 copy-start.1
  1.0 0.9 %copy-done.1 = bf16[2,128,512]{2,1,0:T(8,128)(2,1)S(1)} copy-done((bf16[2,128,512]{2,1,0:T(8,128)(2,1)S(1)}, bf16[2,128,512]{2,1,0:T(8,128)(2,1)}, u32[]{:S(2)}) %copy-start.1) | copy-done | bytes 262168
  1.9 0.0 copy-start.2
  1.9 0.8 %copy-done.2 = bf16[2,128,128]{2,1,0:T(8,128)(2,1)S(1)} copy-done((bf16[2,128,128]{2,1,0:T(8,128)(2,1)S(1)}, bf16[2,128,128]{2,1,0:T(8,128)(2,1)}, u32[]{:S(2)}) %copy-start.2) | copy-done | bytes 65560
  2.7 0.0 copy-start.3
  2.7 0.8 %copy-done.3 = bf16[2,128,128]{2,1,0:T(8,128)(2,1)S(1)} copy-done((bf16[2,128,128]{2,1,0:T(8,128)(2,1)S(1)}, bf16[2,128,128]{2,1,0:T(8,128)(2,1)}, u32[]{:S(2)}) %copy-start.3) | copy-done | bytes 65560
  3.6 0.0 copy-start.4
  3.6 0.7 copy-done.4
  4.3 0.0 copy-start.5
  4.3 0.7 copy-done.5
  5.0 66.0 %triangles.1 = bf16[2,512,128]{2,1,0:T(8,128)(2,1)S(1)} custom-call(bf16[2,512,128]{2,1,0:T(8,128)(2,1)S(1)} %copy-done, s32[2,512]{1,0:T(2,128)S(1)} %copy-done.4, bf16[2,128,512]{2,1,0:T(8,128)(2,1)S(1)} %copy-done.1, bf16[2,128,128]{2,1,0:T(8,128)(2,1)S(1)} %copy-done.2, bf16[2,128,128]{2,1,0:T(8,128)(2,1)S(1)} %copy-done.3, f32[2,2,128]{2,1,0:T(2,128)S(1)} %copy-done.5), custom_call_target="tpu_custom_call" | custom-call | tf_op jit(solution)/shard_map/triangles/pallas_call | solution.py:375
  71.0 0.7 copy.8
Async XLA Ops:
  0.0 0.9 %copy-start = (bf16[2,512,128]{2,1,0:T(8,128)(2,1)S(1)}, bf16[2,512,128]{2,1,0:T(8,128)(2,1)}, u32[]{:S(2)}) copy-start(bf16[2,512,128]{2,1,0:T(8,128)(2,1)} %z_hbm.1) | copy-start | bytes 786436
  1.0 0.9 %copy-start.1 = (bf16[2,128,512]{2,1,0:T(8,128)(2,1)S(1)}, bf16[2,128,512]{2,1,0:T(8,128)(2,1)}, u32[]{:S(2)}) copy-start(bf16[2,128,512]{2,1,0:T(8,128)(2,1)} %we_hbm.1) | copy-start | bytes 786436
  1.9 0.8 %copy-start.2 = (bf16[2,128,128]{2,1,0:T(8,128)(2,1)S(1)}, bf16[2,128,128]{2,1,0:T(8,128)(2,1)}, u32[]{:S(2)}) copy-start(bf16[2,128,128]{2,1,0:T(8,128)(2,1)} %wg_hbm.1) | copy-start | bytes 196612
  2.7 0.8 %copy-start.3 = (bf16[2,128,128]{2,1,0:T(8,128)(2,1)S(1)}, bf16[2,128,128]{2,1,0:T(8,128)(2,1)}, u32[]{:S(2)}) copy-start(bf16[2,128,128]{2,1,0:T(8,128)(2,1)} %wo_hbm.1) | copy-start | bytes 196612
  3.6 0.7 copy-start.4
  4.3 0.7 copy-start.5
